TPU v7x, 256 devices: a whole 4x4x8 slice. The times are simulated.
256 devices in a mesh: gx: 64 (over y, z, core), gy: 4 (over x).
Axes of the slice: x: 4, y: 4, z: 8, core: 2. Of those that a mesh axis runs over, the one named last changes fastest.
Arguments:
- cotangent: float32 [512, 512, 128], P('gx', 'gy'), may hold values from -8 to 8
- capacity: float32 [512, 512, 128], P('gx', 'gy'), may hold values from 0.2 to 2
- conductivity: float32 [512, 512, 128], P('gx', 'gy'), may hold values from 0.5 to 2
- surface_gap: float32 [512, 512], P('gx', 'gy'), may hold values from 0.5 to 2
- transfer_coeff: float32 [2048], replicated, may hold values from 0.25 to 2
- segment_ids: int32 [512, 64], P('gx', 'gy'), may hold values from 0 to 2047
Outputs:
- adjoint: float32 [512, 512, 128], P('gx', 'gy')
- coeff_gradient: float32 [2048], P(('gx', 'gy'))
All inputs are finite; a program needn't handle non-finite values.
Results may differ from a plain program's by a relative error of at most 0.00002.
Values sent between devices are 32-bit elements; how exact they have to be, the bound alone decides.
A program may use at most 128 MiB of HBM per device.

v0:
```python
import jax
import jax.numpy as jnp
from jax import lax
from jax.sharding import PartitionSpec as P

ITERS = 8


LOW_BOUND = 0.2
HIGH_BOUND = 28.0
CENTRE_VALUE = (HIGH_BOUND + LOW_BOUND) / 2.0
HALF_SPREAD = (HIGH_BOUND - LOW_BOUND) / 2.0
SIGMA_RATIO = CENTRE_VALUE / HALF_SPREAD


def extended(cells, sides, width):
    for axis, dim in sides:
        count = lax.axis_size(axis)
        ends = count - 1
        head = lax.slice_in_dim(cells, 0, width, axis=dim)
        tail = lax.slice_in_dim(cells, cells.shape[dim] - width, cells.shape[dim], axis=dim)
        cells = jnp.concatenate(
            [
                lax.ppermute(tail, axis, [(i, (i + 1) % count) for i in range(ends)]),
                cells,
                lax.ppermute(head, axis, [((i + 1) % count, i) for i in range(ends)]),
            ],
            axis=dim,
        )
    return cells


def apply_operator(field, diagonal, cond):
    centre = field[1:-1, 1:-1]
    centre_cond = cond[1:-1, 1:-1]
    accumulated = diagonal[1:-1, 1:-1] * centre
    others = (
        (field[2:, 1:-1], cond[2:, 1:-1]),
        (field[:-2, 1:-1], cond[:-2, 1:-1]),
        (field[1:-1, 2:], cond[1:-1, 2:]),
        (field[1:-1, :-2], cond[1:-1, :-2]),
    )
    for other_field, other_cond in others:
        accumulated = accumulated + 0.5 * (centre_cond + other_cond) * (centre - other_field)
    vertical_field = jnp.pad(centre, ((0, 0), (0, 0), (1, 1)))
    vertical_cond = jnp.pad(centre_cond, ((0, 0), (0, 0), (1, 1)))
    for window in (slice(2, None), slice(0, -2)):
        accumulated = accumulated + 0.5 * (centre_cond + vertical_cond[:, :, window]) * (
            centre - vertical_field[:, :, window]
        )
    return accumulated


def body(cotangent, capacity, conductivity, surface_gap, transfer_coeff, segment_ids):
    blocks = segment_ids.shape[1]
    face_width = surface_gap.shape[1] // blocks
    face_coeff = jnp.repeat(jnp.take(transfer_coeff, segment_ids, axis=0), face_width, axis=1)
    diagonal = capacity + jnp.pad(
        face_coeff[:, :, None], ((0, 0), (0, 0), (0, capacity.shape[2] - 1))
    )
    coeffs = jnp.stack([diagonal, conductivity])
    adjoint = jnp.zeros_like(cotangent)
    residual = cotangent
    direction = residual / CENTRE_VALUE
    ratio_prev = 1.0 / SIGMA_RATIO
    padded = extended(coeffs, (("gx", 1), ("gy", 2)), 1)
    for iteration in range(ITERS):
        adjoint = adjoint + direction
        wide_direction = extended(direction, (("gx", 0), ("gy", 1)), 1)
        residual = residual - apply_operator(wide_direction, padded[0], padded[1])
        if iteration + 1 < ITERS:
            ratio_new = 1.0 / (2.0 * SIGMA_RATIO - ratio_prev)
            direction = (
                ratio_new * ratio_prev * direction + 2.0 * ratio_new / HALF_SPREAD * residual
            )
            ratio_prev = ratio_new
    face_terms = adjoint[:, :, 0] * surface_gap
    block_sums = face_terms.reshape(face_terms.shape[0], blocks, face_width).sum(axis=2)
    partial_value = jax.ops.segment_sum(
        block_sums.reshape(-1), segment_ids.reshape(-1), num_segments=transfer_coeff.shape[0]
    )
    gradient = lax.psum_scatter(partial_value, ("gx", "gy"), scatter_dimension=0, tiled=True)
    return (adjoint, -gradient)


def solution(mesh):
    in_specs = (
        P("gx", "gy", None),
        P("gx", "gy", None),
        P("gx", "gy", None),
        P("gx", "gy"),
        P(),
        P("gx", "gy"),
    )
    out_specs = (P("gx", "gy", None), P(("gx", "gy")))
    return jax.shard_map(body, mesh=mesh, in_specs=in_specs, out_specs=out_specs, check_vma=False)
```

profile of v0, /device:TPU:1, one launch (start us, length us, event | category | flops | bytes accessed | tf_op | source)
XLA Modules:
  0.0 331.2 jit_solution(6894463533862921795)
XLA Ops:
  2.2 5.1 %collective-permute-start.4 = (f32[1,128,128]{1,0,2:T(1,128)S(1)}, f32[1,128,128]{1,0,2:T(1,128)S(1)}, u32[]{:S(2)}, u32[]{:S(2)}) collective-permute-start(f32[1,128,128]{1,0,2:T(1,128)S(1)} %get-tuple-element.59), channel_id=1, source_target_pairs={{4,0},{8,4},{12,8},{16,12},{20,16},{24,20},{28,24},{32,28},{36,32}... | collective-permute-start | bytes 196616 | tf_op jit(solution)/shard_map/ppermute | solution.py:26
  17.1 2.9 collective-permute-done.1
  26.0 3.7 %collective-permute-start.2 = (f32[2,10,1,128]{3,0,2,1:T(2,128)}, f32[2,10,1,128]{3,0,2,1:T(2,128)}, u32[]{:S(2)}, u32[]{:S(2)}) collective-permute-start(f32[2,10,1,128]{3,0,2,1:T(2,128)} %copy.71), channel_id=1, source_target_pairs={{0,1},{1,2},{2,3},{4,5},{5,6},{6,7},{8,9},{9,10},{10,11},{12,13},{... | collective-permute-start | bytes 30728 | tf_op jit(solution)/shard_map/ppermute | solution.py:24
  38.2 4.6 %collective-permute-start.7 = (f32[10,1,128]{2,1,0:T(1,128)S(1)}, f32[10,1,128]{2,1,0:T(1,128)S(1)}, u32[]{:S(2)}, u32[]{:S(2)}) collective-permute-start(f32[10,1,128]{2,1,0:T(1,128)S(1)} %copy.77), channel_id=1, source_target_pairs={{0,1},{1,2},{2,3},{4,5},{5,6},{6,7},{8,9},{9,10},{10,11},{12,13},{... | collective-permute-start | bytes 15368 | tf_op jit(solution)/shard_map/ppermute | solution.py:24
  50.1 5.0 %pad_maximum_fusion = f32[2,10,130,128]{2,1,3,0:T(8,128)S(1)} fusion(f32[2,10,1,128]{2,1,3,0:T(8,128)} %copy.74, f32[2,1,128,128]{2,1,3,0:T(1,128)S(1)} %collective-permute-done.1, f32[1,8,128,128]{2,1,3,0:T(8,128)S(1)} %bitcast.13, f32[1,8,128,128]{2,1,3,0:T(8,128)} %copy-done.4, f32[2,1,128,128]{2,1,3,0:T(1,128)S(1)} %collective-permute-done, ...), kind=kLoop, calls=%fused_computation.2 | loop fusion | flops 1664000 | bytes 2662400 | tf_op jit(solution)/shard_map/concatenate | solution.py:22
  62.2 3.6 %collective-permute-start.9 = (f32[1,128,128]{1,0,2:T(1,128)S(1)}, f32[1,128,128]{1,0,2:T(1,128)S(1)}, u32[]{:S(2)}, u32[]{:S(2)}) collective-permute-start(f32[1,128,128]{1,0,2:T(1,128)S(1)} %get-tuple-element.56), channel_id=1, source_target_pairs={{0,4},{4,8},{8,12},{12,16},{16,20},{20,24},{24,28},{28,32},{32,36}... | collective-permute-start | bytes 196616 | tf_op jit(solution)/shard_map/ppermute | solution.py:24
  73.5 4.0 %collective-permute-start.11 = (f32[10,1,128]{2,1,0:T(1,128)S(1)}, f32[10,1,128]{2,1,0:T(1,128)S(1)}, u32[]{:S(2)}, u32[]{:S(2)}) collective-permute-start(f32[10,1,128]{2,1,0:T(1,128)S(1)} %copy.82), channel_id=1, source_target_pairs={{0,1},{1,2},{2,3},{4,5},{5,6},{6,7},{8,9},{9,10},{10,11},{12,13},{... | collective-permute-start | bytes 15368 | tf_op jit(solution)/shard_map/ppermute | solution.py:24
  80.3 6.2 %multiply_add_fusion.4 = (f32[8,128,128]{1,0,2:T(8,128)S(1)}, f32[8,128,128]{1,0,2:T(8,128)}) fusion(f32[8,128,128]{1,0,2:T(8,128)S(1)} %get-tuple-element.19, f32[8,128,128]{1,0,2:T(8,128)S(1)} %copy.67, f32[8,128,128]{1,0,2:T(8,128)S(1)} %get-tuple-element.21, f32[8,128,128]{1,0,2:T(8,128)} %copy-done.5, f32[8,128,128]{1,0,2:T(8,128)S(1)} %get-tuple-element.20, ...), kind=kLoop, calls=%fused_computation.189 | loop fusion | flops 4456448 | bytes 6432768 | tf_op jit(solution)/shard_map/add | solution.py:74
  88.5 4.8 %collective-permute-start.13 = (f32[1,128,128]{1,0,2:T(1,128)S(1)}, f32[1,128,128]{1,0,2:T(1,128)S(1)}, u32[]{:S(2)}, u32[]{:S(2)}) collective-permute-start(f32[1,128,128]{1,0,2:T(1,128)S(1)} %get-tuple-element.54), channel_id=1, source_target_pairs={{0,4},{4,8},{8,12},{12,16},{16,20},{20,24},{24,28},{28,32},{32,36}... | collective-permute-start | bytes 196616 | tf_op jit(solution)/shard_map/ppermute | solution.py:24
  100.8 4.4 %collective-permute-start.15 = (f32[10,1,128]{2,1,0:T(1,128)S(1)}, f32[10,1,128]{2,1,0:T(1,128)S(1)}, u32[]{:S(2)}, u32[]{:S(2)}) collective-permute-start(f32[10,1,128]{2,1,0:T(1,128)S(1)} %copy.86), channel_id=1, source_target_pairs={{0,1},{1,2},{2,3},{4,5},{5,6},{6,7},{8,9},{9,10},{10,11},{12,13},{... | collective-permute-start | bytes 15368 | tf_op jit(solution)/shard_map/ppermute | solution.py:24
  108.1 6.6 %multiply_add_fusion.3 = (f32[8,128,128]{1,0,2:T(8,128)S(1)}, f32[8,128,128]{1,0,2:T(8,128)}) fusion(f32[8,128,128]{1,0,2:T(8,128)} %get-tuple-element.17, f32[8,128,128]{1,0,2:T(8,128)S(1)} %get-tuple-element.19, f32[8,128,128]{1,0,2:T(8,128)S(1)} %copy.67, f32[8,128,128]{1,0,2:T(8,128)S(1)} %get-tuple-element.21, f32[8,128,128]{1,0,2:T(8,128)} %copy-done.6, ...), kind=kLoop, calls=%fused_computation.188 | loop fusion | flops 4849664 | bytes 6957056 | tf_op jit(solution)/shard_map/add | solution.py:74
  116.7 4.5 %collective-permute-start.17 = (f32[1,128,128]{1,0,2:T(1,128)S(1)}, f32[1,128,128]{1,0,2:T(1,128)S(1)}, u32[]{:S(2)}, u32[]{:S(2)}) collective-permute-start(f32[1,128,128]{1,0,2:T(1,128)S(1)} %get-tuple-element.52), channel_id=1, source_target_pairs={{0,4},{4,8},{8,12},{12,16},{16,20},{20,24},{24,28},{28,32},{32,36}... | collective-permute-start | bytes 196616 | tf_op jit(solution)/shard_map/ppermute | solution.py:24
  128.8 4.4 %collective-permute-start.19 = (f32[10,1,128]{2,1,0:T(1,128)S(1)}, f32[10,1,128]{2,1,0:T(1,128)S(1)}, u32[]{:S(2)}, u32[]{:S(2)}) collective-permute-start(f32[10,1,128]{2,1,0:T(1,128)S(1)} %copy.90), channel_id=1, source_target_pairs={{0,1},{1,2},{2,3},{4,5},{5,6},{6,7},{8,9},{9,10},{10,11},{12,13},{... | collective-permute-start | bytes 15368 | tf_op jit(solution)/shard_map/ppermute | solution.py:24
  136.0 6.6 %multiply_add_fusion.2 = (f32[8,128,128]{1,0,2:T(8,128)S(1)}, f32[8,128,128]{1,0,2:T(8,128)}) fusion(f32[8,128,128]{1,0,2:T(8,128)} %get-tuple-element.15, f32[8,128,128]{1,0,2:T(8,128)} %get-tuple-element.17, f32[8,128,128]{1,0,2:T(8,128)S(1)} %get-tuple-element.19, f32[8,128,128]{1,0,2:T(8,128)S(1)} %copy.67, f32[8,128,128]{1,0,2:T(8,128)S(1)} %get-tuple-element.21, ...), kind=kLoop, calls=%fused_computation.187 | loop fusion | flops 5242880 | bytes 7481344 | tf_op jit(solution)/shard_map/add | solution.py:74
  144.7 4.5 %collective-permute-start.21 = (f32[1,128,128]{1,0,2:T(1,128)S(1)}, f32[1,128,128]{1,0,2:T(1,128)S(1)}, u32[]{:S(2)}, u32[]{:S(2)}) collective-permute-start(f32[1,128,128]{1,0,2:T(1,128)S(1)} %get-tuple-element.50), channel_id=1, source_target_pairs={{0,4},{4,8},{8,12},{12,16},{16,20},{20,24},{24,28},{28,32},{32,36}... | collective-permute-start | bytes 196616 | tf_op jit(solution)/shard_map/ppermute | solution.py:24
  156.7 4.4 %collective-permute-start.23 = (f32[10,1,128]{2,1,0:T(1,128)S(1)}, f32[10,1,128]{2,1,0:T(1,128)S(1)}, u32[]{:S(2)}, u32[]{:S(2)}) collective-permute-start(f32[10,1,128]{2,1,0:T(1,128)S(1)} %copy.94), channel_id=1, source_target_pairs={{0,1},{1,2},{2,3},{4,5},{5,6},{6,7},{8,9},{9,10},{10,11},{12,13},{... | collective-permute-start | bytes 15368 | tf_op jit(solution)/shard_map/ppermute | solution.py:24
  164.0 6.8 %multiply_add_fusion.1 = (f32[8,128,128]{1,0,2:T(8,128)S(1)}, f32[8,128,128]{1,0,2:T(8,128)}) fusion(f32[8,128,128]{1,0,2:T(8,128)} %get-tuple-element.13, f32[8,128,128]{1,0,2:T(8,128)} %get-tuple-element.15, f32[8,128,128]{1,0,2:T(8,128)} %get-tuple-element.17, f32[8,128,128]{1,0,2:T(8,128)S(1)} %get-tuple-element.19, f32[8,128,128]{1,0,2:T(8,128)S(1)} %copy.67, ...), kind=kLoop, calls=%fused_computation.186 | loop fusion | flops 5636096 | bytes 8005632 | tf_op jit(solution)/shard_map/add | solution.py:74
  172.8 4.5 %collective-permute-start.25 = (f32[1,128,128]{1,0,2:T(1,128)S(1)}, f32[1,128,128]{1,0,2:T(1,128)S(1)}, u32[]{:S(2)}, u32[]{:S(2)}) collective-permute-start(f32[1,128,128]{1,0,2:T(1,128)S(1)} %get-tuple-element.48), channel_id=1, source_target_pairs={{0,4},{4,8},{8,12},{12,16},{16,20},{20,24},{24,28},{28,32},{32,36}... | collective-permute-start | bytes 196616 | tf_op jit(solution)/shard_map/ppermute | solution.py:24
  184.8 4.4 %collective-permute-start.27 = (f32[10,1,128]{2,1,0:T(1,128)S(1)}, f32[10,1,128]{2,1,0:T(1,128)S(1)}, u32[]{:S(2)}, u32[]{:S(2)}) collective-permute-start(f32[10,1,128]{2,1,0:T(1,128)S(1)} %copy.98), channel_id=1, source_target_pairs={{0,1},{1,2},{2,3},{4,5},{5,6},{6,7},{8,9},{9,10},{10,11},{12,13},{... | collective-permute-start | bytes 15368 | tf_op jit(solution)/shard_map/ppermute | solution.py:24
  192.1 7.4 %multiply_add_fusion = (f32[8,128,128]{1,0,2:T(8,128)S(1)}, f32[8,128,128]{1,0,2:T(8,128)}) fusion(f32[8,128,128]{1,0,2:T(8,128)} %get-tuple-element.11, f32[8,128,128]{1,0,2:T(8,128)} %get-tuple-element.13, f32[8,128,128]{1,0,2:T(8,128)} %get-tuple-element.15, f32[8,128,128]{1,0,2:T(8,128)} %get-tuple-element.17, f32[8,128,128]{1,0,2:T(8,128)S(1)} %get-tuple-element.19, ...), kind=kLoop, calls=%fused_computation.185 | loop fusion | flops 6029312 | bytes 8529920 | tf_op jit(solution)/shard_map/add | solution.py:74
  201.4 4.5 %collective-permute-start.29 = (f32[1,128,128]{1,0,2:T(1,128)S(1)}, f32[1,128,128]{1,0,2:T(1,128)S(1)}, u32[]{:S(2)}, u32[]{:S(2)}) collective-permute-start(f32[1,128,128]{1,0,2:T(1,128)S(1)} %get-tuple-element.46), channel_id=1, source_target_pairs={{0,4},{4,8},{8,12},{12,16},{16,20},{20,24},{24,28},{28,32},{32,36}... | collective-permute-start | bytes 196616 | tf_op jit(solution)/shard_map/ppermute | solution.py:24
  213.5 4.4 %collective-permute-start.31 = (f32[10,1,128]{2,1,0:T(1,128)S(1)}, f32[10,1,128]{2,1,0:T(1,128)S(1)}, u32[]{:S(2)}, u32[]{:S(2)}) collective-permute-start(f32[10,1,128]{2,1,0:T(1,128)S(1)} %copy.102), channel_id=1, source_target_pairs={{0,1},{1,2},{2,3},{4,5},{5,6},{6,7},{8,9},{9,10},{10,11},{12,13},{... | collective-permute-start | bytes 15368 | tf_op jit(solution)/shard_map/ppermute | solution.py:24
  220.8 7.6 %fusion.8 = f32[8,128,128]{1,0,2:T(8,128)} fusion(f32[8,128,128]{1,0,2:T(8,128)} %get-tuple-element.9, f32[8,128,128]{1,0,2:T(8,128)} %get-tuple-element.25, f32[8,128,128]{1,0,2:T(8,128)} %copy-done.12, f32[10,1,128]{1,0,2:T(8,128)} %copy.103, f32[1,128,128]{1,0,2:T(1,128)S(1)} %collective-permute-done.28, f32[1,128,128]{1,0,2:T(1,128)S(1)} %collective-permute-done.29, ...), kind=kLoop, calls=%fused_computation.22 | loop fusion | flops 7077888 | bytes 8529920 | tf_op jit(solution)/shard_map/add | solution.py:68
  232.7 97.9 %all-reduce.9 = f32[2048]{0:T(1024)S(1)} all-reduce(f32[2048]{0:T(1024)S(1)} %scatter_custom_fusion), channel_id=2, replica_groups=mesh['gx'=64,'gy'=4] {'gx','gy'}, use_global_device_ids=true, to_apply=%region_2.3.clone | all-reduce | flops 2048 | bytes 16384
  (166 shorter events, 116.7 us)
Async XLA Ops:
  2.2 13.7 %collective-permute-start.4 = (f32[1,128,128]{1,0,2:T(1,128)S(1)}, f32[1,128,128]{1,0,2:T(1,128)S(1)}, u32[]{:S(2)}, u32[]{:S(2)}) collective-permute-start(f32[1,128,128]{1,0,2:T(1,128)S(1)} %get-tuple-element.59), channel_id=1, source_target_pairs={{4,0},{8,4},{12,8},{16,12},{20,16},{24,20},{28,24},{32,28},{36,32}... | collective-permute-start | bytes 196616 | tf_op jit(solution)/shard_map/ppermute | solution.py:26
  7.3 8.6 %collective-permute-start.5 = (f32[1,128,128]{1,0,2:T(1,128)S(1)}, f32[1,128,128]{1,0,2:T(1,128)S(1)}, u32[]{:S(2)}, u32[]{:S(2)}) collective-permute-start(f32[1,128,128]{1,0,2:T(1,128)S(1)} %get-tuple-element.58), channel_id=1, source_target_pairs={{0,4},{4,8},{8,12},{12,16},{16,20},{20,24},{24,28},{28,32},{32,36}... | collective-permute-start | bytes 196616 | tf_op jit(solution)/shard_map/ppermute | solution.py:24
  13.7 6.3 %collective-permute-start.1 = (f32[2,1,128,128]{2,1,3,0:T(1,128)S(1)}, f32[2,1,128,128]{2,1,3,0:T(1,128)S(1)}, u32[]{:S(2)}, u32[]{:S(2)}) collective-permute-start(f32[2,1,128,128]{2,1,3,0:T(1,128)S(1)} %get-tuple-element.43), channel_id=1, source_target_pairs={{4,0},{8,4},{12,8},{16,12},{20,16},{24,20},{28,24},{32,28},{36,32}... | collective-permute-start | bytes 393224 | tf_op jit(solution)/shard_map/ppermute | solution.py:26
  26.0 19.7 %collective-permute-start.2 = (f32[2,10,1,128]{3,0,2,1:T(2,128)}, f32[2,10,1,128]{3,0,2,1:T(2,128)}, u32[]{:S(2)}, u32[]{:S(2)}) collective-permute-start(f32[2,10,1,128]{3,0,2,1:T(2,128)} %copy.71), channel_id=1, source_target_pairs={{0,1},{1,2},{2,3},{4,5},{5,6},{6,7},{8,9},{9,10},{10,11},{12,13},{... | collective-permute-start | bytes 30728 | tf_op jit(solution)/shard_map/ppermute | solution.py:24
  32.5 14.8 %collective-permute-start.3 = (f32[2,10,1,128]{3,0,2,1:T(2,128)}, f32[2,10,1,128]{3,0,2,1:T(2,128)}, u32[]{:S(2)}, u32[]{:S(2)}) collective-permute-start(f32[2,10,1,128]{3,0,2,1:T(2,128)} %copy.72), channel_id=1, source_target_pairs={{1,0},{2,1},{3,2},{5,4},{6,5},{7,6},{9,8},{10,9},{11,10},{13,12},{... | collective-permute-start | bytes 30728 | tf_op jit(solution)/shard_map/ppermute | solution.py:26
  36.6 6.2 %collective-permute-start.6 = (f32[10,1,128]{2,1,0:T(1,128)S(1)}, f32[10,1,128]{2,1,0:T(1,128)S(1)}, u32[]{:S(2)}, u32[]{:S(2)}) collective-permute-start(f32[10,1,128]{2,1,0:T(1,128)S(1)} %copy.75), channel_id=1, source_target_pairs={{1,0},{2,1},{3,2},{5,4},{6,5},{7,6},{9,8},{10,9},{11,10},{13,12},{... | collective-permute-start | bytes 15368 | tf_op jit(solution)/shard_map/ppermute | solution.py:26
  38.2 6.0 %collective-permute-start.7 = (f32[10,1,128]{2,1,0:T(1,128)S(1)}, f32[10,1,128]{2,1,0:T(1,128)S(1)}, u32[]{:S(2)}, u32[]{:S(2)}) collective-permute-start(f32[10,1,128]{2,1,0:T(1,128)S(1)} %copy.77), channel_id=1, source_target_pairs={{0,1},{1,2},{2,3},{4,5},{5,6},{6,7},{8,9},{9,10},{10,11},{12,13},{... | collective-permute-start | bytes 15368 | tf_op jit(solution)/shard_map/ppermute | solution.py:24
  70.5 7.0 %collective-permute-start.10 = (f32[10,1,128]{2,1,0:T(1,128)S(1)}, f32[10,1,128]{2,1,0:T(1,128)S(1)}, u32[]{:S(2)}, u32[]{:S(2)}) collective-permute-start(f32[10,1,128]{2,1,0:T(1,128)S(1)} %copy.80), channel_id=1, source_target_pairs={{1,0},{2,1},{3,2},{5,4},{6,5},{7,6},{9,8},{10,9},{11,10},{13,12},{... | collective-permute-start | bytes 15368 | tf_op jit(solution)/shard_map/ppermute | solution.py:26
  86.6 6.8 %collective-permute-start.12 = (f32[1,128,128]{1,0,2:T(1,128)S(1)}, f32[1,128,128]{1,0,2:T(1,128)S(1)}, u32[]{:S(2)}, u32[]{:S(2)}) collective-permute-start(f32[1,128,128]{1,0,2:T(1,128)S(1)} %get-tuple-element.55), channel_id=1, source_target_pairs={{4,0},{8,4},{12,8},{16,12},{20,16},{24,20},{28,24},{32,28},{36,32}... | collective-permute-start | bytes 196616 | tf_op jit(solution)/shard_map/ppermute | solution.py:26
  88.5 6.1 %collective-permute-start.13 = (f32[1,128,128]{1,0,2:T(1,128)S(1)}, f32[1,128,128]{1,0,2:T(1,128)S(1)}, u32[]{:S(2)}, u32[]{:S(2)}) collective-permute-start(f32[1,128,128]{1,0,2:T(1,128)S(1)} %get-tuple-element.54), channel_id=1, source_target_pairs={{0,4},{4,8},{8,12},{12,16},{16,20},{20,24},{24,28},{28,32},{32,36}... | collective-permute-start | bytes 196616 | tf_op jit(solution)/shard_map/ppermute | solution.py:24
  98.0 7.2 %collective-permute-start.14 = (f32[10,1,128]{2,1,0:T(1,128)S(1)}, f32[10,1,128]{2,1,0:T(1,128)S(1)}, u32[]{:S(2)}, u32[]{:S(2)}) collective-permute-start(f32[10,1,128]{2,1,0:T(1,128)S(1)} %copy.84), channel_id=1, source_target_pairs={{1,0},{2,1},{3,2},{5,4},{6,5},{7,6},{9,8},{10,9},{11,10},{13,12},{... | collective-permute-start | bytes 15368 | tf_op jit(solution)/shard_map/ppermute | solution.py:26
  114.8 6.5 %collective-permute-start.16 = (f32[1,128,128]{1,0,2:T(1,128)S(1)}, f32[1,128,128]{1,0,2:T(1,128)S(1)}, u32[]{:S(2)}, u32[]{:S(2)}) collective-permute-start(f32[1,128,128]{1,0,2:T(1,128)S(1)} %get-tuple-element.53), channel_id=1, source_target_pairs={{4,0},{8,4},{12,8},{16,12},{20,16},{24,20},{28,24},{32,28},{36,32}... | collective-permute-start | bytes 196616 | tf_op jit(solution)/shard_map/ppermute | solution.py:26
  116.7 5.9 %collective-permute-start.17 = (f32[1,128,128]{1,0,2:T(1,128)S(1)}, f32[1,128,128]{1,0,2:T(1,128)S(1)}, u32[]{:S(2)}, u32[]{:S(2)}) collective-permute-start(f32[1,128,128]{1,0,2:T(1,128)S(1)} %get-tuple-element.52), channel_id=1, source_target_pairs={{0,4},{4,8},{8,12},{12,16},{16,20},{20,24},{24,28},{28,32},{32,36}... | collective-permute-start | bytes 196616 | tf_op jit(solution)/shard_map/ppermute | solution.py:24
  126.0 7.2 %collective-permute-start.18 = (f32[10,1,128]{2,1,0:T(1,128)S(1)}, f32[10,1,128]{2,1,0:T(1,128)S(1)}, u32[]{:S(2)}, u32[]{:S(2)}) collective-permute-start(f32[10,1,128]{2,1,0:T(1,128)S(1)} %copy.88), channel_id=1, source_target_pairs={{1,0},{2,1},{3,2},{5,4},{6,5},{7,6},{9,8},{10,9},{11,10},{13,12},{... | collective-permute-start | bytes 15368 | tf_op jit(solution)/shard_map/ppermute | solution.py:26
  142.7 6.5 %collective-permute-start.20 = (f32[1,128,128]{1,0,2:T(1,128)S(1)}, f32[1,128,128]{1,0,2:T(1,128)S(1)}, u32[]{:S(2)}, u32[]{:S(2)}) collective-permute-start(f32[1,128,128]{1,0,2:T(1,128)S(1)} %get-tuple-element.51), channel_id=1, source_target_pairs={{4,0},{8,4},{12,8},{16,12},{20,16},{24,20},{28,24},{32,28},{36,32}... | collective-permute-start | bytes 196616 | tf_op jit(solution)/shard_map/ppermute | solution.py:26
  144.7 5.9 %collective-permute-start.21 = (f32[1,128,128]{1,0,2:T(1,128)S(1)}, f32[1,128,128]{1,0,2:T(1,128)S(1)}, u32[]{:S(2)}, u32[]{:S(2)}) collective-permute-start(f32[1,128,128]{1,0,2:T(1,128)S(1)} %get-tuple-element.50), channel_id=1, source_target_pairs={{0,4},{4,8},{8,12},{12,16},{16,20},{20,24},{24,28},{28,32},{32,36}... | collective-permute-start | bytes 196616 | tf_op jit(solution)/shard_map/ppermute | solution.py:24
  153.9 7.2 %collective-permute-start.22 = (f32[10,1,128]{2,1,0:T(1,128)S(1)}, f32[10,1,128]{2,1,0:T(1,128)S(1)}, u32[]{:S(2)}, u32[]{:S(2)}) collective-permute-start(f32[10,1,128]{2,1,0:T(1,128)S(1)} %copy.92), channel_id=1, source_target_pairs={{1,0},{2,1},{3,2},{5,4},{6,5},{7,6},{9,8},{10,9},{11,10},{13,12},{... | collective-permute-start | bytes 15368 | tf_op jit(solution)/shard_map/ppermute | solution.py:26
  170.8 6.5 %collective-permute-start.24 = (f32[1,128,128]{1,0,2:T(1,128)S(1)}, f32[1,128,128]{1,0,2:T(1,128)S(1)}, u32[]{:S(2)}, u32[]{:S(2)}) collective-permute-start(f32[1,128,128]{1,0,2:T(1,128)S(1)} %get-tuple-element.49), channel_id=1, source_target_pairs={{4,0},{8,4},{12,8},{16,12},{20,16},{24,20},{28,24},{32,28},{36,32}... | collective-permute-start | bytes 196616 | tf_op jit(solution)/shard_map/ppermute | solution.py:26
  172.8 5.9 %collective-permute-start.25 = (f32[1,128,128]{1,0,2:T(1,128)S(1)}, f32[1,128,128]{1,0,2:T(1,128)S(1)}, u32[]{:S(2)}, u32[]{:S(2)}) collective-permute-start(f32[1,128,128]{1,0,2:T(1,128)S(1)} %get-tuple-element.48), channel_id=1, source_target_pairs={{0,4},{4,8},{8,12},{12,16},{16,20},{20,24},{24,28},{28,32},{32,36}... | collective-permute-start | bytes 196616 | tf_op jit(solution)/shard_map/ppermute | solution.py:24
  182.0 7.2 %collective-permute-start.26 = (f32[10,1,128]{2,1,0:T(1,128)S(1)}, f32[10,1,128]{2,1,0:T(1,128)S(1)}, u32[]{:S(2)}, u32[]{:S(2)}) collective-permute-start(f32[10,1,128]{2,1,0:T(1,128)S(1)} %copy.96), channel_id=1, source_target_pairs={{1,0},{2,1},{3,2},{5,4},{6,5},{7,6},{9,8},{10,9},{11,10},{13,12},{... | collective-permute-start | bytes 15368 | tf_op jit(solution)/shard_map/ppermute | solution.py:26
  199.5 6.5 %collective-permute-start.28 = (f32[1,128,128]{1,0,2:T(1,128)S(1)}, f32[1,128,128]{1,0,2:T(1,128)S(1)}, u32[]{:S(2)}, u32[]{:S(2)}) collective-permute-start(f32[1,128,128]{1,0,2:T(1,128)S(1)} %get-tuple-element.47), channel_id=1, source_target_pairs={{4,0},{8,4},{12,8},{16,12},{20,16},{24,20},{28,24},{32,28},{36,32}... | collective-permute-start | bytes 196616 | tf_op jit(solution)/shard_map/ppermute | solution.py:26
  201.4 5.9 %collective-permute-start.29 = (f32[1,128,128]{1,0,2:T(1,128)S(1)}, f32[1,128,128]{1,0,2:T(1,128)S(1)}, u32[]{:S(2)}, u32[]{:S(2)}) collective-permute-start(f32[1,128,128]{1,0,2:T(1,128)S(1)} %get-tuple-element.46), channel_id=1, source_target_pairs={{0,4},{4,8},{8,12},{12,16},{16,20},{20,24},{24,28},{28,32},{32,36}... | collective-permute-start | bytes 196616 | tf_op jit(solution)/shard_map/ppermute | solution.py:24
  210.7 7.3 %collective-permute-start.30 = (f32[10,1,128]{2,1,0:T(1,128)S(1)}, f32[10,1,128]{2,1,0:T(1,128)S(1)}, u32[]{:S(2)}, u32[]{:S(2)}) collective-permute-start(f32[10,1,128]{2,1,0:T(1,128)S(1)} %copy.100), channel_id=1, source_target_pairs={{1,0},{2,1},{3,2},{5,4},{6,5},{7,6},{9,8},{10,9},{11,10},{13,12},{... | collective-permute-start | bytes 15368 | tf_op jit(solution)/shard_map/ppermute | solution.py:26
  213.5 5.9 %collective-permute-start.31 = (f32[10,1,128]{2,1,0:T(1,128)S(1)}, f32[10,1,128]{2,1,0:T(1,128)S(1)}, u32[]{:S(2)}, u32[]{:S(2)}) collective-permute-start(f32[10,1,128]{2,1,0:T(1,128)S(1)} %copy.102), channel_id=1, source_target_pairs={{0,1},{1,2},{2,3},{4,5},{5,6},{6,7},{8,9},{9,10},{10,11},{12,13},{... | collective-permute-start | bytes 15368 | tf_op jit(solution)/shard_map/ppermute | solution.py:24
  (27 other events, 293.4 us)
where the time goes:
time: 333 us; the launch traced here: 331 us
  blocking collectives  97.9 us (29%)
  starting transfers between devices  94.4 us (28%)
  local copies, waits for them, and re-layouts  72.3 us (22%)
  other arithmetic  54.4 us (16%)
  waiting for transfers between devices  10.8 us (3%)
    unnamed x1, blocking collectives  97.9 us
    ppermute x16, starting transfers between devices, extended(): lax.ppermute(tail, axis, [(i, (i + 1) % count) for i in range(ends)])  65.2 us
    add x6, other arithmetic, body(): ratio_new * ratio_prev * direction  36.2 us
    ppermute x16, starting transfers between devices, extended(): lax.ppermute(head, axis, [((i + 1) % count, i) for i in range(ends)])  29.2 us
    slice x15, local copies, waits for them, and re-layouts, extended(): head = lax.slice_in_dim(cells, 0, width, axis=dim)  24.7 us
    slice x16, local copies, waits for them, and re-layouts, extended(): lax.slice_in_dim(cells, cells.shape[dim] - width, cells.shape[dim], axis=...  15.4 us
    ppermute x8, local copies, waits for them, and re-layouts, extended(): lax.ppermute(head, axis, [((i + 1) % count, i) for i in range(ends)])  12.7 us
    ppermute x8, local copies, waits for them, and re-layouts, extended(): lax.ppermute(tail, axis, [(i, (i + 1) % count) for i in range(ends)])  11.5 us
  transfers between devices with their start and end apart: 32, of which 7 were waited for; matrix products, arithmetic and copies ran while one was open for 9% of the time, Pallas kernels for 0%

commit v1 on v0

v1 whole, which is shorter than its diff:
```python
import functools

import jax
import jax.numpy as jnp
from jax import lax
from jax.experimental import pallas as pl
from jax.experimental.pallas import tpu as pltpu
from jax.sharding import PartitionSpec as P

MESH = pl.DeviceIdType.MESH
F32 = jnp.float32
ITERS = 8
LOW_BOUND = 0.2
HIGH_BOUND = 28.0
THETA = (HIGH_BOUND + LOW_BOUND) / 2.0
DELTA = (HIGH_BOUND - LOW_BOUND) / 2.0
SIGMA = THETA / DELTA

ROWS, COLS, LANES = 8, 128, 128
DEPTH = 3
SIDE = 8
WIDE = COLS + 2 * SIDE
TALL = ROWS + 2 * DEPTH
OWN_ROWS = pl.ds(DEPTH, ROWS)
OWN_COLS = pl.ds(SIDE, COLS)


def coefficients():
    ratio = 1.0 / SIGMA
    out = []
    for _ in range(ITERS - 1):
        new = 1.0 / (2.0 * SIGMA - ratio)
        out.append((new * ratio, 2.0 * new / DELTA))
        ratio = new
    return out


COEF = coefficients()


def kernel(
    cot, cap, cond, gap_in, tc_in, ids_in,
    out, grad,
    B, C, G, DG, WX, WYp, WYm, WZp, WZm, X, gap, tc, ids, hot, idrow, face, part, got1, row2, got2,
    loc_sem, st_send, st_recv, x_send, x_recv, r_send, r_recv,
):
    gx, gy = lax.axis_index("gx"), lax.axis_index("gy")
    nx, ny = 64, 4
    my_y, my_z, my_c = gx // 16, lax.rem(gx // 2, 8), lax.rem(gx, 2)

    def at(dx, dy):
        return (lax.rem(gx + dx + nx, nx), lax.rem(gy + dy + ny, ny))

    def plane(h):
        return (lax.rem(my_y + h // 4, 4) * 16 + my_z * 2 + my_c, lax.rem(gy + h % 4, 4))

    def column(h):
        return (my_y * 16 + lax.rem(my_z + h // 2, 8) * 2 + lax.rem(my_c + h % 2, 2), gy)

    barrier = pltpu.get_barrier_semaphore()
    around = [(dx, dy) for dx in (-1, 0, 1) for dy in (-1, 0, 1) if dx or dy]
    partners = [at(*d) for d in around] + [plane(h) for h in range(1, 16)] + [column(h) for h in range(1, 16)]
    for dev in partners:
        pl.semaphore_signal(barrier, inc=1, device_id=dev, device_id_type=MESH)

    loads = [
        pltpu.make_async_copy(cot, B.at[OWN_ROWS, OWN_COLS], loc_sem.at[0]),
        pltpu.make_async_copy(cond, C.at[OWN_ROWS, OWN_COLS], loc_sem.at[1]),
        pltpu.make_async_copy(cap, G.at[OWN_ROWS, OWN_COLS], loc_sem.at[2]),
        pltpu.make_async_copy(gap_in, gap, loc_sem.at[3]),
        pltpu.make_async_copy(tc_in, tc, loc_sem.at[4]),
        pltpu.make_async_copy(ids_in, ids, loc_sem.at[5]),
    ]
    for cp in loads:
        cp.start()

    pl.semaphore_wait(barrier, len(partners))

    sends = []
    counter = [0]

    def push(src, dst, dev):
        k = counter[0]
        counter[0] += 1
        cp = pltpu.make_async_remote_copy(
            src, dst, st_send.at[k], st_recv.at[k], device_id=dev, device_id_type=MESH
        )
        cp.start()
        sends.append(cp)
        return cp

    def rows_for(dx, depth_from, count):
        if dx > 0:
            first = ROWS - (depth_from + count - 1)
            return pl.ds(first, count), pl.ds(DEPTH - (depth_from + count - 1), count)
        return pl.ds(depth_from - 1, count), pl.ds(DEPTH + ROWS + depth_from - 1, count)

    def cols_for(dy):
        if dy > 0:
            return pl.ds(COLS - SIDE, SIDE), pl.ds(0, SIDE)
        if dy < 0:
            return pl.ds(0, SIDE), pl.ds(SIDE + COLS, SIDE)
        return pl.ds(0, COLS), OWN_COLS

    near, first, second = [], [], []
    pairs = ((cot, B), (cond, C))
    for src, dst in pairs:
        for dy in (1, -1):
            sc, dc = cols_for(dy)
            near.append(push(src.at[:, sc], dst.at[OWN_ROWS, dc], at(0, dy)))
    for src, dst in pairs:
        for dx in (1, -1):
            sr, dr = rows_for(dx, 1, 2)
            first.append(push(src.at[sr], dst.at[dr, OWN_COLS], at(dx, 0)))
    for src, dst in pairs:
        for dx in (1, -1):
            for dy in (1, -1):
                sr, dr = rows_for(dx, 1, 3)
                sc, dc = cols_for(dy)
                first.append(push(src.at[sr, sc], dst.at[dr, dc], at(dx, dy)))

    for k in (2, 4, 5):
        loads[k].wait()
    lane8 = lax.broadcasted_iota(jnp.int32, (8, LANES), 1)
    lane1 = lax.broadcasted_iota(jnp.int32, (1, LANES), 1)

    def face_row(i, _):
        vec = jnp.zeros((1, LANES), jnp.int32)
        for jb in range(16):
            seg = ids[i, jb]
            value = tc[seg]
            cols = pl.ds(SIDE + 8 * jb, 8)
            G[DEPTH + i, cols, :] = G[DEPTH + i, cols, :] + jnp.where(lane8 == 0, value, 0.0)
            vec = jnp.where(lane1 // 8 == jb, seg, vec)
        idrow[i, :, :] = vec
        return 0

    lax.fori_loop(0, ROWS, face_row, 0)

    for dy in (1, -1):
        sc, dc = cols_for(dy)
        src_cols = pl.ds(SIDE + sc.start, sc.size)
        near.append(push(G.at[OWN_ROWS, src_cols], G.at[OWN_ROWS, dc], at(0, dy)))
    for dx in (1, -1):
        sr, dr = rows_for(dx, 1, 1)
        first.append(push(G.at[pl.ds(DEPTH + sr.start, 1), OWN_COLS], G.at[dr, OWN_COLS], at(dx, 0)))
    for dx in (1, -1):
        for dy in (1, -1):
            sr, dr = rows_for(dx, 1, 2)
            sc, dc = cols_for(dy)
            first.append(
                push(
                    G.at[pl.ds(DEPTH + sr.start, 2), pl.ds(SIDE + sc.start, SIDE)],
                    G.at[dr, dc],
                    at(dx, dy),
                )
            )
    for src, dst in pairs:
        for dx in (1, -1):
            sr, dr = rows_for(dx, 3, 1)
            second.append(push(src.at[sr], dst.at[dr, OWN_COLS], at(dx, 0)))
    for dx in (1, -1):
        sr, dr = rows_for(dx, 2, 1)
        second.append(push(G.at[pl.ds(DEPTH + sr.start, 1), OWN_COLS], G.at[dr, OWN_COLS], at(dx, 0)))

    col = lax.broadcasted_iota(jnp.int32, (WIDE, LANES), 0)
    lane = lax.broadcasted_iota(jnp.int32, (WIDE, LANES), 1)
    left_edge = jnp.logical_and(col == SIDE, gy == 0)
    right_edge = jnp.logical_and(col == SIDE + COLS - 1, gy == ny - 1)

    def setup(r):
        centre = C[r]
        up = jnp.where(jnp.logical_and(r == DEPTH + ROWS - 1, gx == nx - 1), 0.0, C[r + 1])
        down = jnp.where(jnp.logical_and(r == DEPTH, gx == 0), 0.0, C[r - 1])
        right = jnp.where(right_edge, 0.0, pltpu.roll(centre, WIDE - 1, 0))
        left = jnp.where(left_edge, 0.0, pltpu.roll(centre, 1, 0))
        above = jnp.where(lane == LANES - 1, 0.0, pltpu.roll(centre, LANES - 1, 1))
        below = jnp.where(lane == 0, 0.0, pltpu.roll(centre, 1, 1))
        DG[r] = G[r] + (3.0 * centre + 0.5 * ((up + down) + (right + left) + (above + below)))
        WYp[r] = jnp.where(right_edge, 0.0, 0.5 * (centre + right))
        WYm[r] = jnp.where(left_edge, 0.0, 0.5 * (centre + left))
        WZp[r] = jnp.where(lane == LANES - 1, 0.0, 0.5 * (centre + above))
        WZm[r] = jnp.where(lane == 0, 0.0, 0.5 * (centre + below))
        outer = jnp.logical_or(
            jnp.logical_and(r == DEPTH + ROWS - 1, gx == nx - 1), jnp.logical_and(r == DEPTH - 1, gx == 0)
        )
        WX[r] = jnp.where(outer, 0.0, 0.5 * (centre + up))

    def setup_low(r):
        centre = C[r]
        WX[r - 1] = jnp.where(jnp.logical_and(r == DEPTH, gx == 0), 0.0, 0.5 * (centre + C[r - 1]))

    def step(n, r):
        a, beta = COEF[n - 1]
        src = B if n == 1 else X.at[n - 2]
        x = src[r]
        acc = WX[r] * src[r + 1] + WX[r - 1] * src[r - 1]
        acc += WYp[r] * pltpu.roll(x, WIDE - 1, 0) + WYm[r] * pltpu.roll(x, 1, 0)
        acc += WZp[r] * pltpu.roll(x, LANES - 1, 1) + WZm[r] * pltpu.roll(x, 1, 1)
        acc = acc - DG[r] * x
        if n == 1:
            return ((1.0 + a) / THETA + beta) * x + (beta / THETA) * acc
        b = B[r]
        if n == 2:
            return (1.0 + a) * x + (beta - a / THETA) * b + beta * acc
        return (1.0 + a) * x - a * X[n - 3, r] + beta * (b + acc)

    def run(n, rows):
        for i in rows:
            new = step(n, i + DEPTH)
            if n < ITERS - 1:
                X[n - 1, i + DEPTH] = new
            else:
                own = new[SIDE : SIDE + COLS]
                out[i] = own
                acc = jnp.zeros((8, LANES), F32)
                for jb in range(16):
                    piece = jnp.where(lane8 == 0, own[8 * jb : 8 * jb + 8], 0.0)
                    acc = acc + pltpu.roll(piece, 8 * jb, 1, stride=1, stride_axis=0)
                face[i] = jnp.sum(acc, axis=0, keepdims=True) * gap[i : i + 1, :]

    x_copies = {}

    def send_x(n):
        for side, dx, src_row, dst_row in ((0, 1, 5, 0), (1, -1, 2, TALL - 1)):
            cp = pltpu.make_async_remote_copy(
                X.at[n - 2, DEPTH + src_row], X.at[n - 2, dst_row],
                x_send.at[side, n - 2], x_recv.at[side, n - 2],
                device_id=at(dx, 0), device_id_type=MESH,
            )
            cp.start()
            x_copies[side, n] = cp

    loads[0].wait()
    loads[1].wait()
    loads[3].wait()
    for cp in near:
        cp.wait_recv()
    setup_low(1 + DEPTH)
    for i in range(1, 7):
        setup(i + DEPTH)
    run(1, range(1, 7))
    send_x(2)
    run(2, range(2, 6))
    send_x(3)
    run(3, (3, 4))

    sub128 = lax.broadcasted_iota(jnp.int32, (LANES, LANES), 0)

    def one_hot(i, _):
        seg = idrow[i]
        low = ((seg >> 5) & 15) * 8 + (seg & 7)
        hot[i] = jnp.where(sub128 == low, 1.0, 0.0).astype(jnp.bfloat16)
        return 0

    lax.fori_loop(0, ROWS, one_hot, 0)

    for cp in first:
        cp.wait_recv()
    setup_low(-1 + DEPTH)
    for i in (-1, 0, 7, 8):
        setup(i + DEPTH)
    run(1, (-1, 0, 7, 8))
    run(2, (0, 1, 6, 7))
    run(3, (1, 2, 5, 6))
    send_x(4)
    run(4, (2, 3, 4, 5))
    send_x(5)
    run(5, (3, 4))

    for cp in second:
        cp.wait_recv()
    setup_low(-2 + DEPTH)
    for i in (-2, 9):
        setup(i + DEPTH)
    run(1, (-2, 9))
    run(2, (-1, 8))
    run(3, (0, 7))
    run(4, (1, 6))
    run(5, (2, 5))
    run(6, (3, 4))

    for n in (2, 3):
        for side in (0, 1):
            x_copies[side, n].wait_recv()
    run(2, (-2, 9))
    run(3, (-2, -1, 8, 9))
    run(4, (-1, 0, 7, 8))
    run(5, (0, 1, 6, 7))
    run(6, (1, 2, 5, 6))
    run(7, (2, 3, 4, 5))

    for side in (0, 1):
        x_copies[side, 4].wait_recv()
    run(4, (-2, 9))
    run(5, (-1, 8))
    run(6, (0, 7))
    run(7, (1, 6))

    for side in (0, 1):
        x_copies[side, 5].wait_recv()
    run(5, (-2, 9))
    run(6, (-1, 8))
    run(7, (0, 7))

    sub16 = lax.broadcasted_iota(jnp.int32, (16, LANES), 0)
    total = jnp.zeros((48, LANES), F32)
    for i in range(ROWS):
        seg = idrow[i]
        high = (seg >> 9) * 4 + ((seg >> 3) & 3)
        value = jnp.where(sub16 == high, face[i], 0.0)
        v1 = value.astype(jnp.bfloat16).astype(F32)
        v2 = (value - v1).astype(jnp.bfloat16).astype(F32)
        v3 = value - v1 - v2
        left = jnp.concatenate([v1, v2, v3], axis=0).astype(jnp.bfloat16)
        total = total + lax.dot_general(
            left, hot[i], (((1,), (1,)), ((), ())), preferred_element_type=F32
        )
    sums = total[0:16] + total[16:32] + total[32:48]
    for h in range(16):
        part[h] = sums[h : h + 1, :]

    copies = []
    for h in range(1, 16):
        dev = plane(h)
        row = (dev[0] // 16) * 4 + dev[1]
        cp = pltpu.make_async_remote_copy(
            part.at[row], got1.at[h], r_send.at[0, h], r_recv.at[0, h], device_id=dev, device_id_type=MESH
        )
        cp.start()
        copies.append(cp)
    acc = part[my_y * 4 + gy]
    for h, cp in enumerate(copies, 1):
        cp.wait_recv()
        acc = acc + got1[h]
    row2[...] = acc
    more = []
    for h in range(1, 16):
        cp = pltpu.make_async_remote_copy(
            row2, got2.at[h], r_send.at[1, h], r_recv.at[1, h], device_id=column(h), device_id_type=MESH
        )
        cp.start()
        more.append(cp)
    for h, cp in enumerate(more, 1):
        cp.wait_recv()
        acc = acc + got2[h]
    place = (my_z * 2 + my_c) * 8
    spread = jnp.broadcast_to(acc, (8, LANES))
    grad[...] = -pltpu.roll(spread, lax.rem(LANES - place, LANES), 1)

    for cp in sends + list(x_copies.values()) + copies + more:
        cp.wait_send()


def body(cot, cap, cond, gap, tc, ids):
    wide = pltpu.VMEM((TALL, WIDE, LANES), F32)
    n_static = 8 + 8 + 4 + 2 + 2 + 4 + 4 + 2
    adjoint, grad = pl.pallas_call(
        kernel,
        out_shape=(
            jax.ShapeDtypeStruct((ROWS, COLS, LANES), F32),
            jax.ShapeDtypeStruct((8, LANES), F32),
        ),
        in_specs=[pl.BlockSpec(memory_space=pl.ANY)] * 6,
        out_specs=(pl.BlockSpec(memory_space=pltpu.VMEM), pl.BlockSpec(memory_space=pltpu.VMEM)),
        scratch_shapes=[wide] * 9
        + [
            pltpu.VMEM((ITERS - 2, TALL, WIDE, LANES), F32),
            pltpu.VMEM((ROWS, COLS), F32),
            pltpu.SMEM((2048,), F32),
            pltpu.SMEM((ROWS, 16), jnp.int32),
            pltpu.VMEM((ROWS, LANES, LANES), jnp.bfloat16),
            pltpu.VMEM((ROWS, 1, LANES), jnp.int32),
            pltpu.VMEM((ROWS, 1, LANES), F32),
            pltpu.VMEM((16, 1, LANES), F32),
            pltpu.VMEM((16, 1, LANES), F32),
            pltpu.VMEM((1, LANES), F32),
            pltpu.VMEM((16, 1, LANES), F32),
            pltpu.SemaphoreType.DMA((6,)),
            pltpu.SemaphoreType.DMA((n_static,)),
            pltpu.SemaphoreType.DMA((n_static,)),
            pltpu.SemaphoreType.DMA((2, 4)),
            pltpu.SemaphoreType.DMA((2, 4)),
            pltpu.SemaphoreType.DMA((2, 16)),
            pltpu.SemaphoreType.DMA((2, 16)),
        ],
        compiler_params=pltpu.CompilerParams(
            collective_id=0, has_side_effects=True, vmem_limit_bytes=48 * 1024 * 1024
        ),
    )(cot, cap, cond, gap, tc, ids)
    return adjoint, grad[0, 0:8]


def solution(mesh):
    in_specs = (
        P("gx", "gy", None),
        P("gx", "gy", None),
        P("gx", "gy", None),
        P("gx", "gy"),
        P(),
        P("gx", "gy"),
    )
    out_specs = (P("gx", "gy", None), P(("gx", "gy")))
    return jax.shard_map(body, mesh=mesh, in_specs=in_specs, out_specs=out_specs, check_vma=False)
```

time: 333 us -> 42.1 us (0.13)
  blocking collectives: 97.9 us -> 0 us
  starting transfers between devices: 94.4 us -> 0 us
  local copies, waits for them, and re-layouts: 72.3 us -> 6.49 us
  other arithmetic: 54.4 us -> 0 us
  Pallas kernels: 0 us -> 34.6 us
  waiting for transfers between devices: 10.8 us -> 0 us
    unnamed x1 -> x0, blocking collectives: 97.9 us -> none
    ppermute x32 -> x0, starting transfers between devices: 94.4 us -> none  [the longest x16 65.2 us: extended(): lax.ppermute(tail, axis, [(i, (i + 1) % count) for i in range(ends)])]
    add x7 -> x0, other arithmetic: 43.8 us -> none  [the longest x6 36.2 us: body(): ratio_new * ratio_prev * direction]
    slice x32 -> x0, local copies, waits for them, and re-layouts: 40.4 us -> none  [the longest x15 24.7 us: extended(): head = lax.slice_in_dim(cells, 0, width, axis=dim)]
    pallas_call x0 -> x1, Pallas kernels: none -> 34.6 us  [body(): pl.pallas_call(kernel, out_shape=(jax.ShapeDtypeStruct((ROWS, COLS, LANES...]
    ppermute x16 -> x0, local copies, waits for them, and re-layouts: 24.2 us -> none  [the longest x8 12.7 us: extended(): lax.ppermute(head, axis, [((i + 1) % count, i) for i in range(ends)])]
    ppermute x32 -> x0, waiting for transfers between devices: 10.8 us -> none  [the longest x16 7.82 us: extended(): lax.ppermute(tail, axis, [(i, (i + 1) % count) for i in range(ends)])]
    concatenate x9 -> x0, other arithmetic: 7.73 us -> none  [extended(): jnp.concatenate([lax.ppermute(tail, axis, [(i, (i + 1) % count) for i in...]
  transfers between devices with their start and end apart: 32 -> 0, of which waited for: 7 -> 0; matrix products, arithmetic and copies ran while one was open for 9% -> 0% of each run, Pallas kernels for 0% -> 0%
where the time goes in v1:
time: 42.1 us; the launch traced here: 41.8 us
  Pallas kernels  34.6 us (82%)
  local copies, waits for them, and re-layouts  6.49 us (15%)
  between operations  0.65 us (2%)
    pallas_call x1, Pallas kernels, body(): pl.pallas_call(kernel, out_shape=(jax.ShapeDtypeStruct((ROWS, COLS, LANES...  34.6 us
    unnamed x13, local copies, waits for them, and re-layouts  5.98 us

profile of v1, /device:TPU:1, one launch (start us, length us, event | category | flops | bytes accessed | tf_op | source)
XLA Modules:
  0.0 41.8 jit_solution(15176479139521079667)
XLA Ops:
  0.6 0.0 copy-start
  0.6 1.0 %copy-done = f32[8,128,128]{2,1,0:T(8,128)S(1)} copy-done((f32[8,128,128]{2,1,0:T(8,128)S(1)}, f32[8,128,128]{2,1,0:T(8,128)}, u32[]{:S(2)}) %copy-start) | copy-done | bytes 524312
  1.7 0.0 copy-start.1
  1.7 1.0 %copy-done.1 = f32[8,128,128]{2,1,0:T(8,128)S(1)} copy-done((f32[8,128,128]{2,1,0:T(8,128)S(1)}, f32[8,128,128]{2,1,0:T(8,128)}, u32[]{:S(2)}) %copy-start.1) | copy-done | bytes 524312
  2.7 0.0 copy-start.2
  2.7 1.0 %copy-done.2 = f32[8,128,128]{2,1,0:T(8,128)S(1)} copy-done((f32[8,128,128]{2,1,0:T(8,128)S(1)}, f32[8,128,128]{2,1,0:T(8,128)}, u32[]{:S(2)}) %copy-start.2) | copy-done | bytes 524312
  3.8 0.0 copy-start.3
  3.8 0.7 %copy-done.3 = f32[2048]{0:T(1024)S(1)} copy-done((f32[2048]{0:T(1024)S(1)}, f32[2048]{0:T(1024)}, u32[]{:S(2)}) %copy-start.3) | copy-done | bytes 8216
  4.5 0.0 copy-start.4
  4.5 0.7 %copy-done.4 = f32[8,128]{1,0:T(8,128)S(1)} copy-done((f32[8,128]{1,0:T(8,128)S(1)}, f32[8,128]{1,0:T(8,128)}, u32[]{:S(2)}) %copy-start.4) | copy-done | bytes 4120
  5.1 0.0 copy-start.5
  5.1 0.7 %copy-done.5 = s32[8,16]{1,0:T(8,128)S(1)} copy-done((s32[8,16]{1,0:T(8,128)S(1)}, s32[8,16]{1,0:T(8,128)}, u32[]{:S(2)}) %copy-start.5) | copy-done | bytes 536
  5.8 34.6 %shard_map.77 = (f32[8,128,128]{2,1,0:T(8,128)S(1)}, f32[8,128]{1,0:T(8,128)S(1)}) custom-call(f32[8,128,128]{2,1,0:T(8,128)S(1)} %copy-done, f32[8,128,128]{2,1,0:T(8,128)S(1)} %copy-done.1, f32[8,128,128]{2,1,0:T(8,128)S(1)} %copy-done.2, f32[8,128]{1,0:T(8,128)S(1)} %copy-done.4, f32[2048]{0:T(1024)S(1)} %copy-done.3, s32[8,16]{1,0:T(8,128)S(1)} %copy-done.5), custom_call_target="tpu_custom_call" | custom-call | tf_op jit(solution)/shard_map/pallas_call | solution.py:358
  40.5 0.5 %slice_bitcast_fusion = f32[8]{0:T(128)} fusion(f32[8,128]{1,0:T(8,128)S(1)} %get-tuple-element.5), kind=kLoop, calls=%fused_computation | loop fusion | bytes 64 | tf_op jit(solution)/shard_map/squeeze | solution.py:391
  41.0 0.8 %copy.9 = f32[8,128,128]{2,1,0:T(8,128)} copy(f32[8,128,128]{2,1,0:T(8,128)S(1)} %get-tuple-element.8) | data formatting | bytes 1048576
Async XLA Ops:
  0.6 1.0 %copy-start = (f32[8,128,128]{2,1,0:T(8,128)S(1)}, f32[8,128,128]{2,1,0:T(8,128)}, u32[]{:S(2)}) copy-start(f32[8,128,128]{2,1,0:T(8,128)} %cot.1) | copy-start | bytes 1572868
  1.7 1.0 %copy-start.1 = (f32[8,128,128]{2,1,0:T(8,128)S(1)}, f32[8,128,128]{2,1,0:T(8,128)}, u32[]{:S(2)}) copy-start(f32[8,128,128]{2,1,0:T(8,128)} %cap.1) | copy-start | bytes 1572868
  2.7 1.0 %copy-start.2 = (f32[8,128,128]{2,1,0:T(8,128)S(1)}, f32[8,128,128]{2,1,0:T(8,128)}, u32[]{:S(2)}) copy-start(f32[8,128,128]{2,1,0:T(8,128)} %cond.1) | copy-start | bytes 1572868
  3.8 0.7 %copy-start.3 = (f32[2048]{0:T(1024)S(1)}, f32[2048]{0:T(1024)}, u32[]{:S(2)}) copy-start(f32[2048]{0:T(1024)} %tc_in.1) | copy-start | bytes 24580
  4.5 0.7 %copy-start.4 = (f32[8,128]{1,0:T(8,128)S(1)}, f32[8,128]{1,0:T(8,128)}, u32[]{:S(2)}) copy-start(f32[8,128]{1,0:T(8,128)} %gap_in.1) | copy-start | bytes 12292
  5.1 0.7 %copy-start.5 = (s32[8,16]{1,0:T(8,128)S(1)}, s32[8,16]{1,0:T(8,128)}, u32[]{:S(2)}) copy-start(s32[8,16]{1,0:T(8,128)} %ids_in.1) | copy-start | bytes 1540

commit v2 on v1

--- a/solution.py
+++ b/solution.py
@@ -361,7 +361,7 @@
             jax.ShapeDtypeStruct((ROWS, COLS, LANES), F32),
             jax.ShapeDtypeStruct((8, LANES), F32),
         ),
-        in_specs=[pl.BlockSpec(memory_space=pl.ANY)] * 6,
+        in_specs=[pl.BlockSpec(memory_space=pltpu.HBM)] * 6,
         out_specs=(pl.BlockSpec(memory_space=pltpu.VMEM), pl.BlockSpec(memory_space=pltpu.VMEM)),
         scratch_shapes=[wide] * 9
         + [
@@ -387,7 +387,7 @@
         compiler_params=pltpu.CompilerParams(
             collective_id=0, has_side_effects=True, vmem_limit_bytes=48 * 1024 * 1024
         ),
-    )(cot, cap, cond, gap, tc, ids)
+    )(*(pltpu.with_memory_space_constraint(v, pltpu.HBM) for v in (cot, cap, cond, gap, tc, ids)))
     return adjoint, grad[0, 0:8]
 
 

time: 42.1 us -> 37.2 us (0.88)
  local copies, waits for them, and re-layouts: 6.49 us -> 1.31 us
  Pallas kernels: 34.6 us -> 35.2 us
    unnamed x13 -> x1, local copies, waits for them, and re-layouts: 5.98 us -> 0.79 us
    pallas_call x1, Pallas kernels: 34.6 us -> 35.2 us  [body(): pl.pallas_call(kernel, out_shape=(jax.ShapeDtypeStruct((ROWS, COLS, LANES...]
where the time goes in v2:
time: 37.2 us; the launch traced here: 37.1 us
  Pallas kernels  35.2 us (95%)
  local copies, waits for them, and re-layouts  1.31 us (4%)
  between operations  0.64 us (2%)
    pallas_call x1, Pallas kernels, body(): pl.pallas_call(kernel, out_shape=(jax.ShapeDtypeStruct((ROWS, COLS, LANES...  35.2 us
    unnamed x1, local copies, waits for them, and re-layouts  0.79 us

profile of v2, /device:TPU:1, one launch (start us, length us, event | category | flops | bytes accessed | tf_op | source)
XLA Modules:
  0.0 37.1 jit_solution(6615753330931558859)
XLA Ops:
  0.6 35.2 %shard_map.77 = (f32[8,128,128]{2,1,0:T(8,128)S(1)}, f32[8,128]{1,0:T(8,128)S(1)}) custom-call(f32[8,128,128]{2,1,0:T(8,128)} %cot.1, f32[8,128,128]{2,1,0:T(8,128)} %cap.1, f32[8,128,128]{2,1,0:T(8,128)} %cond.1, f32[8,128]{1,0:T(8,128)} %gap_in.1, f32[2048]{0:T(1024)} %tc_in.1, s32[8,16]{1,0:T(8,128)} %ids_in.1), custom_call_target="tpu_custom_call" | custom-call | tf_op jit(solution)/shard_map/pallas_call | solution.py:358
  35.8 0.5 %slice_bitcast_fusion = f32[8]{0:T(128)} fusion(f32[8,128]{1,0:T(8,128)S(1)} %get-tuple-element.5), kind=kLoop, calls=%fused_computation | loop fusion | bytes 64 | tf_op jit(solution)/shard_map/squeeze | solution.py:391
  36.3 0.8 %copy.9 = f32[8,128,128]{2,1,0:T(8,128)} copy(f32[8,128,128]{2,1,0:T(8,128)S(1)} %get-tuple-element.8) | data formatting | bytes 1048576

commit v3 on v2

--- a/solution.py
+++ b/solution.py
@@ -21,6 +21,8 @@
 SIDE = 8
 WIDE = COLS + 2 * SIDE
 TALL = ROWS + 2 * DEPTH
+REACH = ITERS - 1
+SLAB = ROWS + 2 * REACH
 OWN_ROWS = pl.ds(DEPTH, ROWS)
 OWN_COLS = pl.ds(SIDE, COLS)
 
@@ -41,7 +43,8 @@
 def kernel(
     cot, cap, cond, gap_in, tc_in, ids_in,
     out, grad,
-    B, C, G, DG, WX, WYp, WYm, WZp, WZm, X, gap, tc, ids, hot, idrow, face, part, got1, row2, got2,
+    B, C, G, DG, WX, WYp, WYm, WZp, WZm, X, gap, tc, ids, hot, idrow, spread, part, got1, row2, got2,
+    SP, SF, ES, ER, SX,
     loc_sem, st_send, st_recv, x_send, x_recv, r_send, r_recv,
 ):
     gx, gy = lax.axis_index("gx"), lax.axis_index("gy")
@@ -74,8 +77,6 @@
     for cp in loads:
         cp.start()
 
-    pl.semaphore_wait(barrier, len(partners))
-
     sends = []
     counter = [0]
 
@@ -101,6 +102,68 @@
         if dy < 0:
             return pl.ds(0, SIDE), pl.ds(SIDE + COLS, SIDE)
         return pl.ds(0, COLS), OWN_COLS
+
+    for k in (0, 1, 2, 4, 5):
+        loads[k].wait()
+    lane8 = lax.broadcasted_iota(jnp.int32, (8, LANES), 1)
+    lane1 = lax.broadcasted_iota(jnp.int32, (1, LANES), 1)
+
+    def face_row(i, _):
+        vec = jnp.zeros((1, LANES), jnp.int32)
+        for jb in range(16):
+            seg = ids[i, jb]
+            value = tc[seg]
+            cols = pl.ds(SIDE + 8 * jb, 8)
+            G[DEPTH + i, cols, :] = G[DEPTH + i, cols, :] + jnp.where(lane8 == 0, value, 0.0)
+            vec = jnp.where(lane1 == REACH * (jb + 1), seg, vec)
+        idrow[i, :, :] = vec
+        return 0
+
+    lax.fori_loop(0, ROWS, face_row, 0)
+
+    sub8 = lax.broadcasted_iota(jnp.int32, (8, LANES), 0)
+    height = lax.rem(lane8, REACH)
+    low, top = height == 0, height == REACH - 1
+
+    def pack_row(i, _):
+        b = c = g = b7 = c7 = jnp.zeros((8, LANES), F32)
+        for jb in range(16):
+            cols = pl.ds(SIDE + 8 * jb, 8)
+            at0 = REACH * (jb + 1)
+            here = jnp.logical_and(lane8 >= at0, lane8 < at0 + REACH)
+            over = lane8 == at0 + REACH
+            vb = pltpu.roll(B[DEPTH + i, cols, :], at0, 1)
+            vc = pltpu.roll(C[DEPTH + i, cols, :], at0, 1)
+            vg = pltpu.roll(G[DEPTH + i, cols, :], at0, 1)
+            b, c, g = jnp.where(here, vb, b), jnp.where(here, vc, c), jnp.where(here, vg, g)
+            b7, c7 = jnp.where(over, vb, b7), jnp.where(over, vc, c7)
+        b7, c7 = pltpu.roll(b7, LANES - 1, 1), pltpu.roll(c7, LANES - 1, 1)
+        above = jnp.where(top, c7, pltpu.roll(c, LANES - 1, 1))
+        below = jnp.where(low, 0.0, pltpu.roll(c, 1, 1))
+        SP[REACH + i, 0] = b
+        SP[REACH + i, 1] = c
+        SP[REACH + i, 2] = g + c + 0.5 * (above + below)
+        SP[REACH + i, 3] = jnp.where(top, 0.5 * (c + c7) * b7, 0.0)
+        return 0
+
+    lax.fori_loop(0, ROWS, pack_row, 0)
+    lane4 = lax.broadcasted_iota(jnp.int32, (4, 8, LANES), 2)
+    for side, block in ((0, 16), (1, 1)):
+        acc = jnp.zeros((4, 8, LANES), F32)
+        for r in range(ROWS):
+            moved = pltpu.roll(SP[REACH + r], (REACH * (r - block)) % LANES, 2)
+            acc = jnp.where(jnp.logical_and(lane4 >= REACH * r, lane4 < REACH * (r + 1)), moved, acc)
+        ES[side] = acc
+
+    pl.semaphore_wait(barrier, len(partners))
+
+    layer = []
+    for dx in (1, -1):
+        src0, dst0 = (1, 0) if dx > 0 else (0, REACH + ROWS)
+        layer.append(push(SP.at[pl.ds(REACH + src0, REACH)], SP.at[pl.ds(dst0, REACH)], at(dx, 0)))
+    for side, dy in ((0, 1), (1, -1)):
+        for dx in (1, -1, 0):
+            layer.append(push(ES.at[side], ER.at[side, dx + 1], at(dx, dy)))
 
     near, first, second = [], [], []
     pairs = ((cot, B), (cond, C))
@@ -118,24 +181,6 @@
                 sr, dr = rows_for(dx, 1, 3)
                 sc, dc = cols_for(dy)
                 first.append(push(src.at[sr, sc], dst.at[dr, dc], at(dx, dy)))
-
-    for k in (2, 4, 5):
-        loads[k].wait()
-    lane8 = lax.broadcasted_iota(jnp.int32, (8, LANES), 1)
-    lane1 = lax.broadcasted_iota(jnp.int32, (1, LANES), 1)
-
-    def face_row(i, _):
-        vec = jnp.zeros((1, LANES), jnp.int32)
-        for jb in range(16):
-            seg = ids[i, jb]
-            value = tc[seg]
-            cols = pl.ds(SIDE + 8 * jb, 8)
-            G[DEPTH + i, cols, :] = G[DEPTH + i, cols, :] + jnp.where(lane8 == 0, value, 0.0)
-            vec = jnp.where(lane1 // 8 == jb, seg, vec)
-        idrow[i, :, :] = vec
-        return 0
-
-    lax.fori_loop(0, ROWS, face_row, 0)
 
     for dy in (1, -1):
         sc, dc = cols_for(dy)
@@ -211,13 +256,7 @@
             if n < ITERS - 1:
                 X[n - 1, i + DEPTH] = new
             else:
-                own = new[SIDE : SIDE + COLS]
-                out[i] = own
-                acc = jnp.zeros((8, LANES), F32)
-                for jb in range(16):
-                    piece = jnp.where(lane8 == 0, own[8 * jb : 8 * jb + 8], 0.0)
-                    acc = acc + pltpu.roll(piece, 8 * jb, 1, stride=1, stride_axis=0)
-                face[i] = jnp.sum(acc, axis=0, keepdims=True) * gap[i : i + 1, :]
+                out[i] = new[SIDE : SIDE + COLS]
 
     x_copies = {}
 
@@ -231,9 +270,126 @@
             cp.start()
             x_copies[side, n] = cp
 
-    loads[0].wait()
-    loads[1].wait()
     loads[3].wait()
+    pick = [jnp.where(lax.rem(lane8, 8) == sub8, gap[i : i + 1, :], 0.0) for i in range(ROWS)]
+    target = (lax.broadcasted_iota(jnp.int32, (LANES, LANES), 0) // 8 + 1) * REACH
+    place = jnp.where(lax.broadcasted_iota(jnp.int32, (LANES, LANES), 1) == target, 1.0, 0.0).astype(jnp.bfloat16)
+
+    def thirds(value):
+        v1 = value.astype(jnp.bfloat16).astype(F32)
+        v2 = (value - v1).astype(jnp.bfloat16).astype(F32)
+        return jnp.concatenate([v1, v2, value - v1 - v2], axis=0).astype(jnp.bfloat16)
+
+    laid = jnp.dot(thirds(jnp.concatenate(pick, axis=0)), place, preferred_element_type=F32)
+    laid = laid[0:64] + laid[64:128] + laid[128:192]
+    for i in range(ROWS):
+        spread[i] = laid[8 * i : 8 * i + 8, :]
+
+    sub128 = lax.broadcasted_iota(jnp.int32, (LANES, LANES), 0)
+
+    def one_hot(i, _):
+        seg = idrow[i]
+        low = ((seg >> 5) & 15) * 8 + (seg & 7)
+        hot[i] = jnp.where(sub128 == low, 1.0, 0.0).astype(jnp.bfloat16)
+        return 0
+
+    lax.fori_loop(0, ROWS, one_hot, 0)
+
+    for cp in layer:
+        cp.wait_recv()
+    head, tail = lane4 < REACH, jnp.logical_and(lane4 >= 17 * REACH, lane4 < 18 * REACH)
+    for dx in (-1, 0, 1):
+        for r in range(ROWS):
+            q = REACH + r - ROWS * dx
+            if 0 <= q < SLAB:
+                left = pltpu.roll(ER[0, dx + 1], (-REACH * r) % LANES, 2)
+                right = pltpu.roll(ER[1, dx + 1], (REACH * (17 - r)) % LANES, 2)
+                SF[q] = jnp.where(head, left, jnp.where(tail, right, SP[q]))
+
+    def next_col(v):
+        t = pltpu.roll(v, 7, 1)
+        return jnp.where(lax.broadcasted_iota(jnp.int32, v.shape, 1) == 7, pltpu.roll(t, LANES - REACH, 2), t)
+
+    def last_col(v):
+        t = pltpu.roll(v, 1, 1)
+        return jnp.where(lax.broadcasted_iota(jnp.int32, v.shape, 1) == 0, pltpu.roll(t, REACH, 2), t)
+
+    def in_block(shape, block):
+        spot = lax.broadcasted_iota(jnp.int32, shape, 2)
+        return jnp.logical_and(spot >= REACH * block, spot < REACH * (block + 1))
+
+    mid = (SLAB - 2, 8, LANES)
+    rows_ = lax.broadcasted_iota(jnp.int32, mid, 0) + 1
+    subs_ = lax.broadcasted_iota(jnp.int32, mid, 1)
+    high_ = lax.rem(lax.broadcasted_iota(jnp.int32, mid, 2), REACH)
+    off_up = jnp.logical_and(rows_ == REACH + ROWS - 1, gx == nx - 1)
+    off_down = jnp.logical_and(rows_ == REACH, gx == 0)
+    off_right = jnp.logical_and(jnp.logical_and(in_block(mid, 16), subs_ == 7), gy == ny - 1)
+    off_left = jnp.logical_and(jnp.logical_and(in_block(mid, 1), subs_ == 0), gy == 0)
+    sc_ = SF[1 : SLAB - 1, 1]
+    near_cond = [
+        jnp.where(off_up, 0.0, SF[2:SLAB, 1]),
+        jnp.where(off_down, 0.0, SF[0 : SLAB - 2, 1]),
+        jnp.where(off_right, 0.0, next_col(sc_)),
+        jnp.where(off_left, 0.0, last_col(sc_)),
+    ]
+    diag_ = SF[1 : SLAB - 1, 2] + 2.0 * sc_
+    weight = []
+    for off, other in zip((off_up, off_down, off_right, off_left), near_cond):
+        diag_ = diag_ + 0.5 * other
+        weight.append(jnp.where(off, 0.0, 0.5 * (sc_ + other)))
+    weight.append(jnp.where(high_ == REACH - 1, 0.0, 0.5 * (sc_ + pltpu.roll(sc_, LANES - 1, 2))))
+    weight.append(jnp.where(high_ == 0, 0.0, 0.5 * (sc_ + pltpu.roll(sc_, 1, 2))))
+    for k, w in enumerate(weight):
+        SX[k, 1 : SLAB - 1] = w
+    SX[6, 1 : SLAB - 1] = diag_
+
+    for n in range(1, ITERS):
+        a, beta = COEF[n - 1]
+        lo, hi = n, SLAB - n
+
+        def state(m, p, q):
+            return SF[p:q, 0] if m == 1 else SX[5 + m, p:q]
+
+        x = state(n, lo, hi)
+        acc = SX[0, lo:hi] * state(n, lo + 1, hi + 1) + SX[1, lo:hi] * state(n, lo - 1, hi - 1)
+        acc += SX[2, lo:hi] * next_col(x) + SX[3, lo:hi] * last_col(x)
+        acc += SX[4, lo:hi] * pltpu.roll(x, LANES - 1, 2) + SX[5, lo:hi] * pltpu.roll(x, 1, 2)
+        acc = acc - SX[6, lo:hi] * x
+        b = SF[lo:hi, 0]
+        if n == 1:
+            new = ((1.0 + a) / THETA + beta) * x + (beta / THETA) * (acc + SF[lo:hi, 3])
+        elif n == 2:
+            new = (1.0 + a) * x + (beta - a / THETA) * b + beta * acc
+        else:
+            new = (1.0 + a) * x - a * state(n - 1, lo, hi) + beta * (b + acc)
+        if n < ITERS - 1:
+            SX[6 + n, lo:hi] = new
+    faces = jnp.sum(new * spread[...], axis=1, keepdims=True)
+
+    sub16 = lax.broadcasted_iota(jnp.int32, (16, LANES), 0)
+    total = jnp.zeros((48, LANES), F32)
+    for i in range(ROWS):
+        seg = idrow[i]
+        high = (seg >> 9) * 4 + ((seg >> 3) & 3)
+        value = jnp.where(sub16 == high, faces[i], 0.0)
+        left = thirds(value)
+        total = total + lax.dot_general(
+            left, hot[i], (((1,), (1,)), ((), ())), preferred_element_type=F32
+        )
+    sums = total[0:16] + total[16:32] + total[32:48]
+    for h in range(16):
+        part[h] = sums[h : h + 1, :]
+
+    copies = []
+    for h in range(1, 16):
+        dev = plane(h)
+        row = (dev[0] // 16) * 4 + dev[1]
+        cp = pltpu.make_async_remote_copy(
+            part.at[row], got1.at[h], r_send.at[0, h], r_recv.at[0, h], device_id=dev, device_id_type=MESH
+        )
+        cp.start()
+        copies.append(cp)
     for cp in near:
         cp.wait_recv()
     setup_low(1 + DEPTH)
@@ -244,16 +400,6 @@
     run(2, range(2, 6))
     send_x(3)
     run(3, (3, 4))
-
-    sub128 = lax.broadcasted_iota(jnp.int32, (LANES, LANES), 0)
-
-    def one_hot(i, _):
-        seg = idrow[i]
-        low = ((seg >> 5) & 15) * 8 + (seg & 7)
-        hot[i] = jnp.where(sub128 == low, 1.0, 0.0).astype(jnp.bfloat16)
-        return 0
-
-    lax.fori_loop(0, ROWS, one_hot, 0)
 
     for cp in first:
         cp.wait_recv()
@@ -280,55 +426,6 @@
     run(5, (2, 5))
     run(6, (3, 4))
 
-    for n in (2, 3):
-        for side in (0, 1):
-            x_copies[side, n].wait_recv()
-    run(2, (-2, 9))
-    run(3, (-2, -1, 8, 9))
-    run(4, (-1, 0, 7, 8))
-    run(5, (0, 1, 6, 7))
-    run(6, (1, 2, 5, 6))
-    run(7, (2, 3, 4, 5))
-
-    for side in (0, 1):
-        x_copies[side, 4].wait_recv()
-    run(4, (-2, 9))
-    run(5, (-1, 8))
-    run(6, (0, 7))
-    run(7, (1, 6))
-
-    for side in (0, 1):
-        x_copies[side, 5].wait_recv()
-    run(5, (-2, 9))
-    run(6, (-1, 8))
-    run(7, (0, 7))
-
-    sub16 = lax.broadcasted_iota(jnp.int32, (16, LANES), 0)
-    total = jnp.zeros((48, LANES), F32)
-    for i in range(ROWS):
-        seg = idrow[i]
-        high = (seg >> 9) * 4 + ((seg >> 3) & 3)
-        value = jnp.where(sub16 == high, face[i], 0.0)
-        v1 = value.astype(jnp.bfloat16).astype(F32)
-        v2 = (value - v1).astype(jnp.bfloat16).astype(F32)
-        v3 = value - v1 - v2
-        left = jnp.concatenate([v1, v2, v3], axis=0).astype(jnp.bfloat16)
-        total = total + lax.dot_general(
-            left, hot[i], (((1,), (1,)), ((), ())), preferred_element_type=F32
-        )
-    sums = total[0:16] + total[16:32] + total[32:48]
-    for h in range(16):
-        part[h] = sums[h : h + 1, :]
-
-    copies = []
-    for h in range(1, 16):
-        dev = plane(h)
-        row = (dev[0] // 16) * 4 + dev[1]
-        cp = pltpu.make_async_remote_copy(
-            part.at[row], got1.at[h], r_send.at[0, h], r_recv.at[0, h], device_id=dev, device_id_type=MESH
-        )
-        cp.start()
-        copies.append(cp)
     acc = part[my_y * 4 + gy]
     for h, cp in enumerate(copies, 1):
         cp.wait_recv()
@@ -341,12 +438,36 @@
         )
         cp.start()
         more.append(cp)
+
+    for n in (2, 3):
+        for side in (0, 1):
+            x_copies[side, n].wait_recv()
+    run(2, (-2, 9))
+    run(3, (-2, -1, 8, 9))
+    run(4, (-1, 0, 7, 8))
+    run(5, (0, 1, 6, 7))
+    run(6, (1, 2, 5, 6))
+    run(7, (2, 3, 4, 5))
+
+    for side in (0, 1):
+        x_copies[side, 4].wait_recv()
+    run(4, (-2, 9))
+    run(5, (-1, 8))
+    run(6, (0, 7))
+    run(7, (1, 6))
+
+    for side in (0, 1):
+        x_copies[side, 5].wait_recv()
+    run(5, (-2, 9))
+    run(6, (-1, 8))
+    run(7, (0, 7))
+
+    acc = row2[...]
     for h, cp in enumerate(more, 1):
         cp.wait_recv()
         acc = acc + got2[h]
-    place = (my_z * 2 + my_c) * 8
-    spread = jnp.broadcast_to(acc, (8, LANES))
-    grad[...] = -pltpu.roll(spread, lax.rem(LANES - place, LANES), 1)
+    owned = (my_z * 2 + my_c) * 8
+    grad[...] = -pltpu.roll(jnp.broadcast_to(acc, (8, LANES)), lax.rem(LANES - owned, LANES), 1)
 
     for cp in sends + list(x_copies.values()) + copies + more:
         cp.wait_send()
@@ -354,7 +475,7 @@
 
 def body(cot, cap, cond, gap, tc, ids):
     wide = pltpu.VMEM((TALL, WIDE, LANES), F32)
-    n_static = 8 + 8 + 4 + 2 + 2 + 4 + 4 + 2
+    n_static = 8 + 4 + 4 + 8 + 2 + 2 + 4 + 4 + 2
     adjoint, grad = pl.pallas_call(
         kernel,
         out_shape=(
@@ -371,11 +492,16 @@
             pltpu.SMEM((ROWS, 16), jnp.int32),
             pltpu.VMEM((ROWS, LANES, LANES), jnp.bfloat16),
             pltpu.VMEM((ROWS, 1, LANES), jnp.int32),
-            pltpu.VMEM((ROWS, 1, LANES), F32),
+            pltpu.VMEM((ROWS, 8, LANES), F32),
             pltpu.VMEM((16, 1, LANES), F32),
             pltpu.VMEM((16, 1, LANES), F32),
             pltpu.VMEM((1, LANES), F32),
             pltpu.VMEM((16, 1, LANES), F32),
+            pltpu.VMEM((SLAB, 4, 8, LANES), F32),
+            pltpu.VMEM((SLAB, 4, 8, LANES), F32),
+            pltpu.VMEM((2, 4, 8, LANES), F32),
+            pltpu.VMEM((2, 3, 4, 8, LANES), F32),
+            pltpu.VMEM((13, SLAB, 8, LANES), F32),
             pltpu.SemaphoreType.DMA((6,)),
             pltpu.SemaphoreType.DMA((n_static,)),
             pltpu.SemaphoreType.DMA((n_static,)),

time: 37.2 us -> 31 us (0.83)
  the two profiles are of different devices: /device:TPU:1 before, /device:TPU:6 now
where the time goes in v3:
time: 31 us; the launch traced here: 30.9 us
  Pallas kernels  28.9 us (93%)
  local copies, waits for them, and re-layouts  1.31 us (4%)
  between operations  0.64 us (2%)
    pallas_call x1, Pallas kernels, body(): pl.pallas_call(kernel, out_shape=(jax.ShapeDtypeStruct((ROWS, COLS, LANES...  28.9 us
    unnamed x1, local copies, waits for them, and re-layouts  0.79 us

profile of v3, /device:TPU:6, one launch (start us, length us, event | category | flops | bytes accessed | tf_op | source)
XLA Modules:
  0.0 30.9 jit_solution(2206784842779554117)
XLA Ops:
  0.6 28.9 %shard_map.77 = (f32[8,128,128]{2,1,0:T(8,128)S(1)}, f32[8,128]{1,0:T(8,128)S(1)}) custom-call(f32[8,128,128]{2,1,0:T(8,128)} %cot.1, f32[8,128,128]{2,1,0:T(8,128)} %cap.1, f32[8,128,128]{2,1,0:T(8,128)} %cond.1, f32[8,128]{1,0:T(8,128)} %gap_in.1, f32[2048]{0:T(1024)} %tc_in.1, s32[8,16]{1,0:T(8,128)} %ids_in.1), custom_call_target="tpu_custom_call" | custom-call | tf_op jit(solution)/shard_map/pallas_call | solution.py:479
  29.6 0.5 %slice_bitcast_fusion = f32[8]{0:T(128)} fusion(f32[8,128]{1,0:T(8,128)S(1)} %get-tuple-element.5), kind=kLoop, calls=%fused_computation | loop fusion | bytes 64 | tf_op jit(solution)/shard_map/squeeze | solution.py:517
  30.1 0.8 %copy.9 = f32[8,128,128]{2,1,0:T(8,128)} copy(f32[8,128,128]{2,1,0:T(8,128)S(1)} %get-tuple-element.8) | data formatting | bytes 1048576

commit v4 on v3

--- a/solution.py
+++ b/solution.py
@@ -44,7 +44,7 @@
     cot, cap, cond, gap_in, tc_in, ids_in,
     out, grad,
     B, C, G, DG, WX, WYp, WYm, WZp, WZm, X, gap, tc, ids, hot, idrow, spread, part, got1, row2, got2,
-    SP, SF, ES, ER, SX,
+    SP, SF, SB, RB, ES, ER, SX,
     loc_sem, st_send, st_recv, x_send, x_recv, r_send, r_recv,
 ):
     gx, gy = lax.axis_index("gx"), lax.axis_index("gy")
@@ -59,6 +59,9 @@
 
     def column(h):
         return (my_y * 16 + lax.rem(my_z + h // 2, 8) * 2 + lax.rem(my_c + h % 2, 2), gy)
+
+    plane_order = sorted(range(1, 16), key=lambda h: -min(h // 4, 4 - h // 4) - min(h % 4, 4 - h % 4))
+    column_order = sorted(range(1, 16), key=lambda h: -min(h // 2, 8 - h // 2) - (h % 2) / 2)
 
     barrier = pltpu.get_barrier_semaphore()
     around = [(dx, dy) for dx in (-1, 0, 1) for dy in (-1, 0, 1) if dx or dy]
@@ -140,30 +143,41 @@
         b7, c7 = pltpu.roll(b7, LANES - 1, 1), pltpu.roll(c7, LANES - 1, 1)
         above = jnp.where(top, c7, pltpu.roll(c, LANES - 1, 1))
         below = jnp.where(low, 0.0, pltpu.roll(c, 1, 1))
-        SP[REACH + i, 0] = b
-        SP[REACH + i, 1] = c
-        SP[REACH + i, 2] = g + c + 0.5 * (above + below)
-        SP[REACH + i, 3] = jnp.where(top, 0.5 * (c + c7) * b7, 0.0)
+        SP[i, 0] = b
+        SP[i, 1] = c
+        SP[i, 2] = g + c + 0.5 * (above + below)
+        SP[i, 3] = jnp.where(top, 0.5 * (c + c7) * b7, 0.0)
         return 0
 
     lax.fori_loop(0, ROWS, pack_row, 0)
-    lane4 = lax.broadcasted_iota(jnp.int32, (4, 8, LANES), 2)
+    for side, row0 in ((0, 1), (1, 0)):
+        terms = jnp.zeros((8, LANES), F32)
+        for k in range(REACH):
+            for arr in range(3):
+                SB[side, 3 * k + arr] = SP[row0 + k, arr]
+            terms = jnp.where(height == k, pltpu.roll(SP[row0 + k, 3], (k - REACH + 1) % LANES, 1), terms)
+        SB[side, 3 * REACH] = terms
+    HALF = REACH * ROWS
     for side, block in ((0, 16), (1, 1)):
-        acc = jnp.zeros((4, 8, LANES), F32)
+        tiles = [jnp.zeros((8, LANES), F32)] * 2
         for r in range(ROWS):
-            moved = pltpu.roll(SP[REACH + r], (REACH * (r - block)) % LANES, 2)
-            acc = jnp.where(jnp.logical_and(lane4 >= REACH * r, lane4 < REACH * (r + 1)), moved, acc)
-        ES[side] = acc
+            for arr, tile, to, width in ((0, 0, REACH * r, REACH), (1, 0, HALF + REACH * r, REACH),
+                                         (2, 1, REACH * r, REACH), (3, 1, HALF + r, 1)):
+                start = REACH * block + (REACH - 1 if arr == 3 else 0)
+                moved = pltpu.roll(SP[r, arr], (to - start) % LANES, 1)
+                tiles[tile] = jnp.where(jnp.logical_and(lane8 >= to, lane8 < to + width), moved, tiles[tile])
+        ES[side, 0], ES[side, 1] = tiles
 
     pl.semaphore_wait(barrier, len(partners))
 
     layer = []
     for dx in (1, -1):
-        src0, dst0 = (1, 0) if dx > 0 else (0, REACH + ROWS)
-        layer.append(push(SP.at[pl.ds(REACH + src0, REACH)], SP.at[pl.ds(dst0, REACH)], at(dx, 0)))
+        for side, dy in ((0, 1), (1, -1)):
+            layer.append(push(ES.at[side], ER.at[side, dx + 1], at(dx, dy)))
+    for side, dx in ((0, 1), (1, -1)):
+        layer.append(push(SB.at[side], RB.at[side], at(dx, 0)))
     for side, dy in ((0, 1), (1, -1)):
-        for dx in (1, -1, 0):
-            layer.append(push(ES.at[side], ER.at[side, dx + 1], at(dx, dy)))
+        layer.append(push(ES.at[side], ER.at[side, 1], at(0, dy)))
 
     near, first, second = [], [], []
     pairs = ((cot, B), (cond, C))
@@ -171,10 +185,12 @@
         for dy in (1, -1):
             sc, dc = cols_for(dy)
             near.append(push(src.at[:, sc], dst.at[OWN_ROWS, dc], at(0, dy)))
-    for src, dst in pairs:
-        for dx in (1, -1):
-            sr, dr = rows_for(dx, 1, 2)
-            first.append(push(src.at[sr], dst.at[dr, OWN_COLS], at(dx, 0)))
+    first2 = []
+    for depth, group in ((1, first), (2, first2)):
+        for src, dst in pairs:
+            for dx in (1, -1):
+                sr, dr = rows_for(dx, depth, 1)
+                group.append(push(src.at[sr], dst.at[dr, OWN_COLS], at(dx, 0)))
     for src, dst in pairs:
         for dx in (1, -1):
             for dy in (1, -1):
@@ -188,12 +204,12 @@
         near.append(push(G.at[OWN_ROWS, src_cols], G.at[OWN_ROWS, dc], at(0, dy)))
     for dx in (1, -1):
         sr, dr = rows_for(dx, 1, 1)
-        first.append(push(G.at[pl.ds(DEPTH + sr.start, 1), OWN_COLS], G.at[dr, OWN_COLS], at(dx, 0)))
+        first2.append(push(G.at[pl.ds(DEPTH + sr.start, 1), OWN_COLS], G.at[dr, OWN_COLS], at(dx, 0)))
     for dx in (1, -1):
         for dy in (1, -1):
             sr, dr = rows_for(dx, 1, 2)
             sc, dc = cols_for(dy)
-            first.append(
+            first2.append(
                 push(
                     G.at[pl.ds(DEPTH + sr.start, 2), pl.ds(SIDE + sc.start, SIDE)],
                     G.at[dr, dc],
@@ -208,53 +224,68 @@
         sr, dr = rows_for(dx, 2, 1)
         second.append(push(G.at[pl.ds(DEPTH + sr.start, 1), OWN_COLS], G.at[dr, OWN_COLS], at(dx, 0)))
 
-    col = lax.broadcasted_iota(jnp.int32, (WIDE, LANES), 0)
-    lane = lax.broadcasted_iota(jnp.int32, (WIDE, LANES), 1)
-    left_edge = jnp.logical_and(col == SIDE, gy == 0)
-    right_edge = jnp.logical_and(col == SIDE + COLS - 1, gy == ny - 1)
-
-    def setup(r):
-        centre = C[r]
-        up = jnp.where(jnp.logical_and(r == DEPTH + ROWS - 1, gx == nx - 1), 0.0, C[r + 1])
-        down = jnp.where(jnp.logical_and(r == DEPTH, gx == 0), 0.0, C[r - 1])
-        right = jnp.where(right_edge, 0.0, pltpu.roll(centre, WIDE - 1, 0))
-        left = jnp.where(left_edge, 0.0, pltpu.roll(centre, 1, 0))
+    inner = (SIDE, SIDE + COLS, SIDE + 8, SIDE + COLS - 8)
+    inner2 = (SIDE + 8, SIDE + COLS - 8, SIDE + 16, SIDE + COLS - 16)
+    rims = ((0, SIDE + 16, 0, SIDE + 8), (SIDE + COLS - 16, WIDE, SIDE + COLS - 8, WIDE))
+    rims2 = ((0, SIDE + 24, 0, SIDE + 16), (SIDE + COLS - 24, WIDE, SIDE + COLS - 16, WIDE))
+
+    def window(span):
+        lo, hi, start, stop = span
+        return pl.ds(lo, hi - lo), hi - lo, pl.ds(start, stop - start), lambda v: v[start - lo : stop - lo]
+
+    def setup(r, span=(0, WIDE, 0, WIDE)):
+        read, width, keep, cut = window(span)
+        col = lax.broadcasted_iota(jnp.int32, (span[3] - span[2], LANES), 0) + span[2]
+        lane = lax.broadcasted_iota(jnp.int32, (span[3] - span[2], LANES), 1)
+        left_edge = jnp.logical_and(col == SIDE, gy == 0)
+        right_edge = jnp.logical_and(col == SIDE + COLS - 1, gy == ny - 1)
+        line = C[r, read, :]
+        centre = cut(line)
+        up = jnp.where(jnp.logical_and(r == DEPTH + ROWS - 1, gx == nx - 1), 0.0, C[r + 1, keep, :])
+        down = jnp.where(jnp.logical_and(r == DEPTH, gx == 0), 0.0, C[r - 1, keep, :])
+        right = jnp.where(right_edge, 0.0, cut(pltpu.roll(line, width - 1, 0)))
+        left = jnp.where(left_edge, 0.0, cut(pltpu.roll(line, 1, 0)))
         above = jnp.where(lane == LANES - 1, 0.0, pltpu.roll(centre, LANES - 1, 1))
         below = jnp.where(lane == 0, 0.0, pltpu.roll(centre, 1, 1))
-        DG[r] = G[r] + (3.0 * centre + 0.5 * ((up + down) + (right + left) + (above + below)))
-        WYp[r] = jnp.where(right_edge, 0.0, 0.5 * (centre + right))
-        WYm[r] = jnp.where(left_edge, 0.0, 0.5 * (centre + left))
-        WZp[r] = jnp.where(lane == LANES - 1, 0.0, 0.5 * (centre + above))
-        WZm[r] = jnp.where(lane == 0, 0.0, 0.5 * (centre + below))
+        DG[r, keep, :] = G[r, keep, :] + (
+            3.0 * centre + 0.5 * ((up + down) + (right + left) + (above + below))
+        )
+        WYp[r, keep, :] = jnp.where(right_edge, 0.0, 0.5 * (centre + right))
+        WYm[r, keep, :] = jnp.where(left_edge, 0.0, 0.5 * (centre + left))
+        WZp[r, keep, :] = jnp.where(lane == LANES - 1, 0.0, 0.5 * (centre + above))
+        WZm[r, keep, :] = jnp.where(lane == 0, 0.0, 0.5 * (centre + below))
         outer = jnp.logical_or(
             jnp.logical_and(r == DEPTH + ROWS - 1, gx == nx - 1), jnp.logical_and(r == DEPTH - 1, gx == 0)
         )
-        WX[r] = jnp.where(outer, 0.0, 0.5 * (centre + up))
-
-    def setup_low(r):
-        centre = C[r]
-        WX[r - 1] = jnp.where(jnp.logical_and(r == DEPTH, gx == 0), 0.0, 0.5 * (centre + C[r - 1]))
-
-    def step(n, r):
+        WX[r, keep, :] = jnp.where(outer, 0.0, 0.5 * (centre + up))
+
+    def setup_low(r, keep=pl.ds(0, WIDE)):
+        WX[r - 1, keep, :] = jnp.where(
+            jnp.logical_and(r == DEPTH, gx == 0), 0.0, 0.5 * (C[r, keep, :] + C[r - 1, keep, :])
+        )
+
+    def step(n, r, span):
         a, beta = COEF[n - 1]
+        read, width, keep, cut = window(span)
         src = B if n == 1 else X.at[n - 2]
-        x = src[r]
-        acc = WX[r] * src[r + 1] + WX[r - 1] * src[r - 1]
-        acc += WYp[r] * pltpu.roll(x, WIDE - 1, 0) + WYm[r] * pltpu.roll(x, 1, 0)
-        acc += WZp[r] * pltpu.roll(x, LANES - 1, 1) + WZm[r] * pltpu.roll(x, 1, 1)
-        acc = acc - DG[r] * x
+        line = src[r, read, :]
+        x = cut(line)
+        acc = WX[r, keep, :] * src[r + 1, keep, :] + WX[r - 1, keep, :] * src[r - 1, keep, :]
+        acc += WYp[r, keep, :] * cut(pltpu.roll(line, width - 1, 0)) + WYm[r, keep, :] * cut(pltpu.roll(line, 1, 0))
+        acc += WZp[r, keep, :] * pltpu.roll(x, LANES - 1, 1) + WZm[r, keep, :] * pltpu.roll(x, 1, 1)
+        acc = acc - DG[r, keep, :] * x
         if n == 1:
             return ((1.0 + a) / THETA + beta) * x + (beta / THETA) * acc
-        b = B[r]
+        b = B[r, keep, :]
         if n == 2:
             return (1.0 + a) * x + (beta - a / THETA) * b + beta * acc
-        return (1.0 + a) * x - a * X[n - 3, r] + beta * (b + acc)
-
-    def run(n, rows):
+        return (1.0 + a) * x - a * X[n - 3, r, keep, :] + beta * (b + acc)
+
+    def run(n, rows, span=(0, WIDE, 0, WIDE)):
         for i in rows:
-            new = step(n, i + DEPTH)
+            new = step(n, i + DEPTH, span)
             if n < ITERS - 1:
-                X[n - 1, i + DEPTH] = new
+                X[n - 1, i + DEPTH, pl.ds(span[2], span[3] - span[2]), :] = new
             else:
                 out[i] = new[SIDE : SIDE + COLS]
 
@@ -295,16 +326,34 @@
 
     lax.fori_loop(0, ROWS, one_hot, 0)
 
+    setup_low(1 + DEPTH, pl.ds(inner[2], inner[3] - inner[2]))
+    for i in range(1, 7):
+        setup(i + DEPTH, inner)
+    run(1, range(1, 7), inner)
+    run(2, range(2, 6), inner2)
+
     for cp in layer:
         cp.wait_recv()
-    head, tail = lane4 < REACH, jnp.logical_and(lane4 >= 17 * REACH, lane4 < 18 * REACH)
+    head = lane8 < REACH
+    tail = jnp.logical_and(lane8 >= 17 * REACH, lane8 < 18 * REACH)
     for dx in (-1, 0, 1):
         for r in range(ROWS):
             q = REACH + r - ROWS * dx
-            if 0 <= q < SLAB:
-                left = pltpu.roll(ER[0, dx + 1], (-REACH * r) % LANES, 2)
-                right = pltpu.roll(ER[1, dx + 1], (REACH * (17 - r)) % LANES, 2)
-                SF[q] = jnp.where(head, left, jnp.where(tail, right, SP[q]))
+            if not 0 <= q < SLAB:
+                continue
+            for arr, tile, start in ((0, 0, REACH * r), (1, 0, HALF + REACH * r), (2, 1, REACH * r), (3, 1, HALF + r)):
+                skip = REACH - 1 if arr == 3 else 0
+                if dx == 0:
+                    own = SP[r, arr]
+                elif arr < 3:
+                    own = RB[0 if dx > 0 else 1, 3 * (r - (1 if dx > 0 else 0)) + arr]
+                else:
+                    k = r - (1 if dx > 0 else 0)
+                    own = pltpu.roll(RB[0 if dx > 0 else 1, 3 * REACH], REACH - 1 - k, 1)
+                left = pltpu.roll(ER[0, dx + 1, tile], (skip - start) % LANES, 1)
+                right = pltpu.roll(ER[1, dx + 1, tile], (17 * REACH + skip - start) % LANES, 1)
+                row = jnp.where(head, left, jnp.where(tail, right, own))
+                SF[q, arr] = jnp.where(top, row, 0.0) if arr == 3 else row
 
     def next_col(v):
         t = pltpu.roll(v, 7, 1)
@@ -382,7 +431,7 @@
         part[h] = sums[h : h + 1, :]
 
     copies = []
-    for h in range(1, 16):
+    for h in plane_order:
         dev = plane(h)
         row = (dev[0] // 16) * 4 + dev[1]
         cp = pltpu.make_async_remote_copy(
@@ -392,26 +441,37 @@
         copies.append(cp)
     for cp in near:
         cp.wait_recv()
-    setup_low(1 + DEPTH)
-    for i in range(1, 7):
-        setup(i + DEPTH)
-    run(1, range(1, 7))
+    for rim in rims:
+        setup_low(1 + DEPTH, pl.ds(rim[2], rim[3] - rim[2]))
+        for i in range(1, 7):
+            setup(i + DEPTH, rim)
+        run(1, range(1, 7), rim)
     send_x(2)
-    run(2, range(2, 6))
+    for rim in rims2:
+        run(2, range(2, 6), rim)
     send_x(3)
     run(3, (3, 4))
 
     for cp in first:
         cp.wait_recv()
+    setup_low(DEPTH)
+    for i in (0, 7):
+        setup(i + DEPTH)
+    run(1, (0, 7))
+    run(2, (1, 6))
+    run(3, (2, 5))
+    send_x(4)
+    for cp in first2:
+        cp.wait_recv()
     setup_low(-1 + DEPTH)
-    for i in (-1, 0, 7, 8):
+    for i in (-1, 8):
         setup(i + DEPTH)
-    run(1, (-1, 0, 7, 8))
-    run(2, (0, 1, 6, 7))
-    run(3, (1, 2, 5, 6))
-    send_x(4)
-    run(4, (2, 3, 4, 5))
+    run(1, (-1, 8))
+    run(2, (0, 7))
+    run(3, (1, 6))
+    run(4, (2, 5))
     send_x(5)
+    run(4, (3, 4))
     run(5, (3, 4))
 
     for cp in second:
@@ -427,12 +487,12 @@
     run(6, (3, 4))
 
     acc = part[my_y * 4 + gy]
-    for h, cp in enumerate(copies, 1):
+    for h, cp in zip(plane_order, copies):
         cp.wait_recv()
         acc = acc + got1[h]
     row2[...] = acc
     more = []
-    for h in range(1, 16):
+    for h in column_order:
         cp = pltpu.make_async_remote_copy(
             row2, got2.at[h], r_send.at[1, h], r_recv.at[1, h], device_id=column(h), device_id_type=MESH
         )
@@ -463,7 +523,7 @@
     run(7, (0, 7))
 
     acc = row2[...]
-    for h, cp in enumerate(more, 1):
+    for h, cp in zip(column_order, more):
         cp.wait_recv()
         acc = acc + got2[h]
     owned = (my_z * 2 + my_c) * 8
@@ -475,7 +535,7 @@
 
 def body(cot, cap, cond, gap, tc, ids):
     wide = pltpu.VMEM((TALL, WIDE, LANES), F32)
-    n_static = 8 + 4 + 4 + 8 + 2 + 2 + 4 + 4 + 2
+    n_static = 8 + 4 + 8 + 8 + 2 + 2 + 4 + 4 + 2
     adjoint, grad = pl.pallas_call(
         kernel,
         out_shape=(
@@ -497,10 +557,12 @@
             pltpu.VMEM((16, 1, LANES), F32),
             pltpu.VMEM((1, LANES), F32),
             pltpu.VMEM((16, 1, LANES), F32),
+            pltpu.VMEM((ROWS, 4, 8, LANES), F32),
             pltpu.VMEM((SLAB, 4, 8, LANES), F32),
-            pltpu.VMEM((SLAB, 4, 8, LANES), F32),
-            pltpu.VMEM((2, 4, 8, LANES), F32),
-            pltpu.VMEM((2, 3, 4, 8, LANES), F32),
+            pltpu.VMEM((2, 3 * REACH + 1, 8, LANES), F32),
+            pltpu.VMEM((2, 3 * REACH + 1, 8, LANES), F32),
+            pltpu.VMEM((2, 2, 8, LANES), F32),
+            pltpu.VMEM((2, 3, 2, 8, LANES), F32),
             pltpu.VMEM((13, SLAB, 8, LANES), F32),
             pltpu.SemaphoreType.DMA((6,)),
             pltpu.SemaphoreType.DMA((n_static,)),

time: 31 us -> 29.6 us (0.955)
  the two profiles are of different devices: /device:TPU:6 before, /device:TPU:1 now
where the time goes in v4:
time: 29.6 us; the launch traced here: 29.5 us
  Pallas kernels  27.6 us (93%)
  local copies, waits for them, and re-layouts  1.31 us (4%)
  between operations  0.64 us (2%)
    pallas_call x1, Pallas kernels, body(): pl.pallas_call(kernel, out_shape=(jax.ShapeDtypeStruct((ROWS, COLS, LANES...  27.6 us
    unnamed x1, local copies, waits for them, and re-layouts  0.79 us

profile of v4, /device:TPU:1, one launch (start us, length us, event | category | flops | bytes accessed | tf_op | source)
XLA Modules:
  0.0 29.5 jit_solution(14310010482181848080)
XLA Ops:
  0.6 27.6 %shard_map.77 = (f32[8,128,128]{2,1,0:T(8,128)S(1)}, f32[8,128]{1,0:T(8,128)S(1)}) custom-call(f32[8,128,128]{2,1,0:T(8,128)} %cot.1, f32[8,128,128]{2,1,0:T(8,128)} %cap.1, f32[8,128,128]{2,1,0:T(8,128)} %cond.1, f32[8,128]{1,0:T(8,128)} %gap_in.1, f32[2048]{0:T(1024)} %tc_in.1, s32[8,16]{1,0:T(8,128)} %ids_in.1), custom_call_target="tpu_custom_call" | custom-call | tf_op jit(solution)/shard_map/pallas_call | solution.py:539
  28.2 0.5 %slice_bitcast_fusion = f32[8]{0:T(128)} fusion(f32[8,128]{1,0:T(8,128)S(1)} %get-tuple-element.5), kind=kLoop, calls=%fused_computation | loop fusion | bytes 64 | tf_op jit(solution)/shard_map/squeeze | solution.py:579
  28.7 0.8 %copy.9 = f32[8,128,128]{2,1,0:T(8,128)} copy(f32[8,128,128]{2,1,0:T(8,128)S(1)} %get-tuple-element.8) | data formatting | bytes 1048576

commit v5 on v4

--- a/solution.py
+++ b/solution.py
@@ -430,15 +430,16 @@
     for h in range(16):
         part[h] = sums[h : h + 1, :]
 
-    copies = []
+    def all_in(box, sem):
+        pltpu.make_async_copy(box.at[pl.ds(1, 15)], box.at[pl.ds(1, 15)], sem).wait()
+
     for h in plane_order:
         dev = plane(h)
         row = (dev[0] // 16) * 4 + dev[1]
         cp = pltpu.make_async_remote_copy(
-            part.at[row], got1.at[h], r_send.at[0, h], r_recv.at[0, h], device_id=dev, device_id_type=MESH
+            part.at[row], got1.at[h], r_send.at[0], r_recv.at[0], device_id=dev, device_id_type=MESH
         )
         cp.start()
-        copies.append(cp)
     for cp in near:
         cp.wait_recv()
     for rim in rims:
@@ -486,18 +487,14 @@
     run(5, (2, 5))
     run(6, (3, 4))
 
-    acc = part[my_y * 4 + gy]
-    for h, cp in zip(plane_order, copies):
-        cp.wait_recv()
-        acc = acc + got1[h]
+    all_in(got1, r_recv.at[0])
+    acc = part[my_y * 4 + gy] + jnp.sum(got1[1:16], axis=0)
     row2[...] = acc
-    more = []
     for h in column_order:
         cp = pltpu.make_async_remote_copy(
-            row2, got2.at[h], r_send.at[1, h], r_recv.at[1, h], device_id=column(h), device_id_type=MESH
+            row2, got2.at[h], r_send.at[1], r_recv.at[1], device_id=column(h), device_id_type=MESH
         )
         cp.start()
-        more.append(cp)
 
     for n in (2, 3):
         for side in (0, 1):
@@ -509,6 +506,9 @@
     run(6, (1, 2, 5, 6))
     run(7, (2, 3, 4, 5))
 
+    for cp in sends:
+        cp.wait_send()
+    all_in(got1, r_send.at[0])
     for side in (0, 1):
         x_copies[side, 4].wait_recv()
     run(4, (-2, 9))
@@ -516,21 +516,20 @@
     run(6, (0, 7))
     run(7, (1, 6))
 
+    for cp in x_copies.values():
+        cp.wait_send()
     for side in (0, 1):
         x_copies[side, 5].wait_recv()
     run(5, (-2, 9))
     run(6, (-1, 8))
     run(7, (0, 7))
 
-    acc = row2[...]
-    for h, cp in zip(column_order, more):
-        cp.wait_recv()
-        acc = acc + got2[h]
+    all_in(got2, r_recv.at[1])
+    acc = row2[...] + jnp.sum(got2[1:16], axis=0)
     owned = (my_z * 2 + my_c) * 8
     grad[...] = -pltpu.roll(jnp.broadcast_to(acc, (8, LANES)), lax.rem(LANES - owned, LANES), 1)
 
-    for cp in sends + list(x_copies.values()) + copies + more:
-        cp.wait_send()
+    all_in(got2, r_send.at[1])
 
 
 def body(cot, cap, cond, gap, tc, ids):
@@ -569,8 +568,8 @@
             pltpu.SemaphoreType.DMA((n_static,)),
             pltpu.SemaphoreType.DMA((2, 4)),
             pltpu.SemaphoreType.DMA((2, 4)),
-            pltpu.SemaphoreType.DMA((2, 16)),
-            pltpu.SemaphoreType.DMA((2, 16)),
+            pltpu.SemaphoreType.DMA((2,)),
+            pltpu.SemaphoreType.DMA((2,)),
         ],
         compiler_params=pltpu.CompilerParams(
             collective_id=0, has_side_effects=True, vmem_limit_bytes=48 * 1024 * 1024

time: 29.6 us -> 28.9 us (0.976)
  Pallas kernels: 27.6 us -> 26.9 us
    pallas_call x1, Pallas kernels: 27.6 us -> 26.9 us  [body(): pl.pallas_call(kernel, out_shape=(jax.ShapeDtypeStruct((ROWS, COLS, LANES...]
where the time goes in v5:
time: 28.9 us; the launch traced here: 28.8 us
  Pallas kernels  26.9 us (93%)
  local copies, waits for them, and re-layouts  1.31 us (5%)
  between operations  0.64 us (2%)
    pallas_call x1, Pallas kernels, body(): pl.pallas_call(kernel, out_shape=(jax.ShapeDtypeStruct((ROWS, COLS, LANES...  26.9 us
    unnamed x1, local copies, waits for them, and re-layouts  0.79 us

profile of v5, /device:TPU:1, one launch (start us, length us, event | category | flops | bytes accessed | tf_op | source)
XLA Modules:
  0.0 28.8 jit_solution(5728540074586089162)
XLA Ops:
  0.6 26.9 %shard_map.77 = (f32[8,128,128]{2,1,0:T(8,128)S(1)}, f32[8,128]{1,0:T(8,128)S(1)}) custom-call(f32[8,128,128]{2,1,0:T(8,128)} %cot.1, f32[8,128,128]{2,1,0:T(8,128)} %cap.1, f32[8,128,128]{2,1,0:T(8,128)} %cond.1, f32[8,128]{1,0:T(8,128)} %gap_in.1, f32[2048]{0:T(1024)} %tc_in.1, s32[8,16]{1,0:T(8,128)} %ids_in.1), custom_call_target="tpu_custom_call" | custom-call | tf_op jit(solution)/shard_map/pallas_call | solution.py:538
  27.5 0.5 %slice_bitcast_fusion = f32[8]{0:T(128)} fusion(f32[8,128]{1,0:T(8,128)S(1)} %get-tuple-element.5), kind=kLoop, calls=%fused_computation | loop fusion | bytes 64 | tf_op jit(solution)/shard_map/squeeze | solution.py:578
  28.0 0.8 %copy.9 = f32[8,128,128]{2,1,0:T(8,128)} copy(f32[8,128,128]{2,1,0:T(8,128)S(1)} %get-tuple-element.8) | data formatting | bytes 1048576

commit v6 on v5

--- a/solution.py
+++ b/solution.py
@@ -65,7 +65,7 @@
 
     barrier = pltpu.get_barrier_semaphore()
     around = [(dx, dy) for dx in (-1, 0, 1) for dy in (-1, 0, 1) if dx or dy]
-    partners = [at(*d) for d in around] + [plane(h) for h in range(1, 16)] + [column(h) for h in range(1, 16)]
+    partners = [at(*d) for d in sorted(around, key=lambda d: -abs(d[0]) - abs(d[1]))] + [column(h) for h in column_order] + [plane(h) for h in plane_order]
     for dev in partners:
         pl.semaphore_signal(barrier, inc=1, device_id=dev, device_id_type=MESH)
 
@@ -181,16 +181,15 @@
 
     near, first, second = [], [], []
     pairs = ((cot, B), (cond, C))
+    first2 = []
     for src, dst in pairs:
         for dy in (1, -1):
             sc, dc = cols_for(dy)
             near.append(push(src.at[:, sc], dst.at[OWN_ROWS, dc], at(0, dy)))
-    first2 = []
-    for depth, group in ((1, first), (2, first2)):
-        for src, dst in pairs:
-            for dx in (1, -1):
-                sr, dr = rows_for(dx, depth, 1)
-                group.append(push(src.at[sr], dst.at[dr, OWN_COLS], at(dx, 0)))
+    for dy in (1, -1):
+        sc, dc = cols_for(dy)
+        src_cols = pl.ds(SIDE + sc.start, sc.size)
+        near.append(push(G.at[OWN_ROWS, src_cols], G.at[OWN_ROWS, dc], at(0, dy)))
     for src, dst in pairs:
         for dx in (1, -1):
             for dy in (1, -1):
@@ -198,13 +197,6 @@
                 sc, dc = cols_for(dy)
                 first.append(push(src.at[sr, sc], dst.at[dr, dc], at(dx, dy)))
 
-    for dy in (1, -1):
-        sc, dc = cols_for(dy)
-        src_cols = pl.ds(SIDE + sc.start, sc.size)
-        near.append(push(G.at[OWN_ROWS, src_cols], G.at[OWN_ROWS, dc], at(0, dy)))
-    for dx in (1, -1):
-        sr, dr = rows_for(dx, 1, 1)
-        first2.append(push(G.at[pl.ds(DEPTH + sr.start, 1), OWN_COLS], G.at[dr, OWN_COLS], at(dx, 0)))
     for dx in (1, -1):
         for dy in (1, -1):
             sr, dr = rows_for(dx, 1, 2)
@@ -216,6 +208,14 @@
                     at(dx, dy),
                 )
             )
+    for depth, group in ((1, first), (2, first2)):
+        for src, dst in pairs:
+            for dx in (1, -1):
+                sr, dr = rows_for(dx, depth, 1)
+                group.append(push(src.at[sr], dst.at[dr, OWN_COLS], at(dx, 0)))
+    for dx in (1, -1):
+        sr, dr = rows_for(dx, 1, 1)
+        first2.append(push(G.at[pl.ds(DEPTH + sr.start, 1), OWN_COLS], G.at[dr, OWN_COLS], at(dx, 0)))
     for src, dst in pairs:
         for dx in (1, -1):
             sr, dr = rows_for(dx, 3, 1)
@@ -527,7 +527,7 @@
     all_in(got2, r_recv.at[1])
     acc = row2[...] + jnp.sum(got2[1:16], axis=0)
     owned = (my_z * 2 + my_c) * 8
-    grad[...] = -pltpu.roll(jnp.broadcast_to(acc, (8, LANES)), lax.rem(LANES - owned, LANES), 1)
+    grad[...] = -pltpu.roll(jnp.broadcast_to(acc, (8, LANES)), lax.rem(LANES - owned, LANES), 1)[0, 0:8]
 
     all_in(got2, r_send.at[1])
 
@@ -539,7 +539,7 @@
         kernel,
         out_shape=(
             jax.ShapeDtypeStruct((ROWS, COLS, LANES), F32),
-            jax.ShapeDtypeStruct((8, LANES), F32),
+            jax.ShapeDtypeStruct((8,), F32),
         ),
         in_specs=[pl.BlockSpec(memory_space=pltpu.HBM)] * 6,
         out_specs=(pl.BlockSpec(memory_space=pltpu.VMEM), pl.BlockSpec(memory_space=pltpu.VMEM)),
@@ -575,7 +575,7 @@
             collective_id=0, has_side_effects=True, vmem_limit_bytes=48 * 1024 * 1024
         ),
     )(*(pltpu.with_memory_space_constraint(v, pltpu.HBM) for v in (cot, cap, cond, gap, tc, ids)))
-    return adjoint, grad[0, 0:8]
+    return adjoint, grad
 
 
 def solution(mesh):

time: 28.9 us -> 29.2 us (1.010)
    unnamed x1 -> x2, local copies, waits for them, and re-layouts: 0.79 us -> 1.31 us
    squeeze x1 -> x0, local copies, waits for them, and re-layouts: 0.51 us -> none  [body(): return (adjoint, grad[0, 0:8])]
where the time goes in v6:
time: 29.2 us; the launch traced here: 29.1 us
  Pallas kernels  27.1 us (93%)
  local copies, waits for them, and re-layouts  1.31 us (4%)
  between operations  0.64 us (2%)
    pallas_call x1, Pallas kernels, body(): pl.pallas_call(kernel, out_shape=(jax.ShapeDtypeStruct((ROWS, COLS, LANES...  27.1 us
    unnamed x2, local copies, waits for them, and re-layouts  1.31 us

profile of v6, /device:TPU:1, one launch (start us, length us, event | category | flops | bytes accessed | tf_op | source)
XLA Modules:
  0.0 29.1 jit_solution(13372630928783515974)
XLA Ops:
  0.6 27.1 %shard_map.77 = (f32[8,128,128]{2,1,0:T(8,128)S(1)}, f32[8]{0:T(128)S(1)}) custom-call(f32[8,128,128]{2,1,0:T(8,128)} %cot.1, f32[8,128,128]{2,1,0:T(8,128)} %cap.1, f32[8,128,128]{2,1,0:T(8,128)} %cond.1, f32[8,128]{1,0:T(8,128)} %gap_in.1, f32[2048]{0:T(1024)} %tc_in.1, s32[8,16]{1,0:T(8,128)} %ids_in.1), custom_call_target="tpu_custom_call" | custom-call | tf_op jit(solution)/shard_map/pallas_call | solution.py:538
  27.8 0.8 %copy.10 = f32[8,128,128]{2,1,0:T(8,128)} copy(f32[8,128,128]{2,1,0:T(8,128)S(1)} %get-tuple-element.4) | data formatting | bytes 1048576
  28.5 0.5 %copy.11 = f32[8]{0:T(128)} copy(f32[8]{0:T(128)S(1)} %get-tuple-element.5) | data formatting | bytes 64
